TPU v7x, 256 devices: a whole 4x4x8 slice. The times are simulated.
256 devices in a mesh: group: 4 (over y), dev: 64 (over z, x, core).
Axes of the slice: x: 4, y: 4, z: 8, core: 2. Of those that a mesh axis runs over, the one named last changes fastest.
Arguments:
- tokens: bfloat16 [256, 512, 1024], P(('group', 'dev')), may hold values from -12 to 12
- pair_list: int32 [256, 2], P(('group', 'dev')), may hold values from 0 to 255, as said below
- confidence: int32 [256, 2, 512], P(('group', 'dev')), may hold values from 1 to 32
- w_embed: bfloat16 [1024, 768], replicated, may hold values from -0.1875 to 0.1875
- w_query: bfloat16 [768, 768], replicated, may hold values from -0.21875 to 0.21875
- w_key: bfloat16 [768, 768], replicated, may hold values from -0.21875 to 0.21875
- w_value: bfloat16 [768, 768], replicated, may hold values from -0.21875 to 0.21875
- w_out: bfloat16 [768, 768], replicated, may hold values from -0.21875 to 0.21875
- norm_gain: float32 [768], replicated, may hold values from 0.25 to 1.75
- w_head: bfloat16 [768, 3456], replicated, may hold values from -0.21875 to 0.21875
Outputs:
- merged_maps: bfloat16 [256, 512, 3456], P(('group', 'dev'))
Inputs may be any that keep to these rules, and one draw needn't show every extreme that they name: `pair_list`: each pair names two different images whose indices differ from the pair's own index by at most one.
All inputs are finite; a program needn't handle non-finite values.
Results may differ from a plain program's by a relative error of at most 0.012.
Values may be sent and summed in bfloat16 or wider, within the bound.
A program may use at most 128 MiB of HBM per device.

v0:
```python
import jax
import jax.numpy as jnp
from jax import lax
from jax.sharding import PartitionSpec as P

HEADS = 12
HEAD_DIM = 64


def extended(block, sides, width):
    for axis, dim in sides:
        count = lax.axis_size(axis)
        forward = [(i, i + 1) for i in range(count - 1)]
        backward = [(target, source) for source, target in forward]
        low = lax.ppermute(
            lax.slice_in_dim(block, block.shape[dim] - width, None, axis=dim), axis, forward
        )
        high = lax.ppermute(lax.slice_in_dim(block, 0, width, axis=dim), axis, backward)
        block = jnp.concatenate([low, block, high], axis=dim)
    return block


def passed_along(block, axis, distance):
    devices = range(lax.axis_size(axis))
    route = [(i - distance, i) for i in devices if i - distance in devices]
    return lax.ppermute(block, axis, route)


def cross_branch(x_q, x_kv, w_query, w_key, w_value, w_out, norm_gain, w_head):
    tok = x_q.shape[0]
    q = jnp.dot(x_q, w_query, preferred_element_type=jnp.float32).astype(jnp.bfloat16)
    k = jnp.dot(x_kv, w_key, preferred_element_type=jnp.float32).astype(jnp.bfloat16)
    v = jnp.dot(x_kv, w_value, preferred_element_type=jnp.float32).astype(jnp.bfloat16)

    def split(m):
        return m.reshape(tok, HEADS // 4, 4, HEAD_DIM).transpose(1, 2, 0, 3)

    def attend(blocks):
        qb, kb, vb = blocks
        scores = (
            jnp.einsum("htd,hsd->hts", qb, kb, preferred_element_type=jnp.float32) / HEAD_DIM**0.5
        )
        top = jnp.max(scores, axis=-1, keepdims=True)
        expo = jnp.exp(scores - top)
        probs = (expo / jnp.sum(expo, axis=-1, keepdims=True)).astype(jnp.bfloat16)
        return jnp.einsum("hts,hsd->htd", probs, vb, preferred_element_type=jnp.float32)

    ctx = lax.map(attend, (split(q), split(k), split(v)))
    context = ctx.transpose(2, 0, 1, 3).reshape(tok, HEADS * HEAD_DIM).astype(jnp.bfloat16)
    mixed = x_q.astype(jnp.float32) + jnp.dot(context, w_out, preferred_element_type=jnp.float32)
    center = mixed - jnp.mean(mixed, axis=-1, keepdims=True)
    spread = jnp.mean(center * center, axis=-1, keepdims=True)
    normed = (center / jnp.sqrt(spread + 1e-06) * norm_gain).astype(jnp.bfloat16)
    return jnp.dot(normed, w_head, preferred_element_type=jnp.float32)


def on_device(
    tokens, pair_list, confidence, w_embed, w_query, w_key, w_value, w_out, norm_gain, w_head
):
    own_index = lax.axis_index(("group", "dev"))
    slot_a = pair_list[0, 0] - own_index + 1
    slot_b = pair_list[0, 1] - own_index + 1
    nearby = extended(tokens, ((("group", "dev"), 0),), 1)
    raw_a = lax.dynamic_index_in_dim(nearby, slot_a, 0, keepdims=False)
    raw_b = lax.dynamic_index_in_dim(nearby, slot_b, 0, keepdims=False)
    first = jnp.dot(raw_a, w_embed, preferred_element_type=jnp.float32).astype(jnp.bfloat16)
    second = jnp.dot(raw_b, w_embed, preferred_element_type=jnp.float32).astype(jnp.bfloat16)
    out_a = cross_branch(first, second, w_query, w_key, w_value, w_out, norm_gain, w_head)
    out_b = cross_branch(second, first, w_query, w_key, w_value, w_out, norm_gain, w_head)
    conf_a = confidence[0, 0].astype(jnp.float32)
    conf_b = confidence[0, 1].astype(jnp.float32)
    slots = jnp.arange(3, dtype=jnp.int32)
    pick_a = (slots == slot_a).astype(jnp.float32)
    pick_b = (slots == slot_b).astype(jnp.float32)
    terms = (
        pick_a[:, None, None] * (conf_a[:, None] * out_a)[None]
        + pick_b[:, None, None] * (conf_b[:, None] * out_b)[None]
    )
    sums = pick_a[:, None] * conf_a[None] + pick_b[:, None] * conf_b[None]
    from_upper = passed_along((terms[0], sums[0]), ("group", "dev"), -1)
    from_lower = passed_along((terms[2], sums[2]), ("group", "dev"), 1)
    total = terms[1] + from_upper[0] + from_lower[0]
    weight = sums[1] + from_upper[1] + from_lower[1]
    return (total / jnp.maximum(weight, 1.0)[:, None]).astype(jnp.bfloat16)[None]


def solution(mesh):
    in_specs = (
        P(("group", "dev"), None, None),
        P(("group", "dev"), None),
        P(("group", "dev"), None, None),
        P(),
        P(),
        P(),
        P(),
        P(),
        P(),
        P(),
    )
    out_specs = P(("group", "dev"), None, None)
    return jax.shard_map(
        on_device, mesh=mesh, in_specs=in_specs, out_specs=out_specs, check_vma=False
    )
```

profile of v0, /device:TPU:24, one launch (start us, length us, event | category | flops | bytes accessed | tf_op | source)
XLA Modules:
  0.0 214.7 jit_solution(16217299176249337314)
XLA Ops:
  0.0 2.0 collective-permute-start
  2.1 9.6 %collective-permute-start.1 = (bf16[1,512,1024]{2,1,0:T(8,128)(2,1)}, bf16[1,512,1024]{2,1,0:T(8,128)(2,1)S(1)}, u32[]{:S(2)}, u32[]{:S(2)}) collective-permute-start(bf16[1,512,1024]{2,1,0:T(8,128)(2,1)} %param.14), channel_id=1, source_target_pairs={{1,0},{2,1},{3,2},{4,3},{5,4},{6,5},{7,6},{8,7},{9,8},{10,9},{11,1... | collective-permute-start | bytes 3145736 | tf_op jit(solution)/shard_map/ppermute | solution.py:18
  11.6 1.3 fusion.110
  14.3 0.8 slice_convert_fusion.1
  15.0 7.5 %collective-permute-done = bf16[1,512,1024]{2,1,0:T(8,128)(2,1)} collective-permute-done((bf16[1,512,1024]{2,1,0:T(8,128)(2,1)}, bf16[1,512,1024]{2,1,0:T(8,128)(2,1)}, u32[]{:S(2)}, u32[]{:S(2)}) %collective-permute-start) | collective-permute-done | bytes 1048608 | tf_op jit(solution)/shard_map/ppermute | solution.py:15
  22.5 1.3 constant_dynamic-update-slice_fusion.2
  23.8 1.3 constant_dynamic-update-slice_fusion.1
  25.1 0.0 collective-permute-done.1
  25.1 0.1 constant_dynamic-update-slice_fusion
  25.2 1.0 convolution_convert_fusion.6
  26.2 0.0 copy-start.4
  26.2 1.0 convolution_convert_fusion.7
  27.2 0.6 copy-done.4
  27.7 0.8 convolution_convert_fusion
  28.5 0.8 copy-done.3
  29.3 1.7 convolution_convert_fusion.5
  31.0 1.7 convolution_convert_fusion.2
  32.6 0.8 convolution_convert_fusion.3
  33.4 1.7 convolution_convert_fusion.1
  35.1 0.8 convolution_convert_fusion.4
  35.9 0.3 copy.26
  36.2 2.3 %copy.25 = bf16[512,768]{0,1:T(8,128)(2,1)} copy(bf16[512,768]{1,0:T(8,128)(2,1)} %convolution_convert_fusion.1) | data formatting | bytes 1572864 | tf_op jit(solution)/shard_map/convert_element_type | solution.py:32
  38.5 1.4 copy.21
  39.9 2.3 %copy.24 = bf16[512,768]{0,1:T(8,128)(2,1)} copy(bf16[512,768]{1,0:T(8,128)(2,1)} %convolution_convert_fusion.2) | data formatting | bytes 1572864 | tf_op jit(solution)/shard_map/convert_element_type | solution.py:31
  42.2 0.9 broadcast.75.clone
  43.2 23.6 %while.21 = (s32[]{:T(128)}, bf16[3,4,512,64]{2,3,1,0:T(8,128)(2,1)}, bf16[3,4,512,64]{2,3,1,0:T(8,128)(2,1)}, bf16[3,4,512,64]{2,3,1,0:T(8,128)(2,1)}, bf16[3,4,512,64]{2,3,1,0:T(8,128)(2,1)S(1)}, /*index=5*/s32[]{:T(128)}) while((s32[]{:T(128)}, bf16[3,4,512,64]{2,3,1,0:T(8,128)(2,1)}, bf16[3,4,512,64]{2,3,1,0:T(8,128)(2,1)}, ...), condition=%wide.region_9.10_spmd, body=%wide.region_6.9_spmd.sunk | while | flops 273678848 | bytes 9717837 | solution.py:48
  43.2 4.5 %fusion.151 = (f32[4,512]{1,0:T(4,128)S(1)}, f32[4,512,512]{1,2,0:T(8,128)}) fusion(bf16[3,4,512,64]{2,3,1,0:T(8,128)(2,1)} %get-tuple-element.185, s32[]{:T(128)S(6)} %copy.35, bf16[3,4,512,64]{2,3,1,0:T(8,128)(2,1)} %get-tuple-element.184), kind=kOutput, calls=%fused_computation.101.clone.1 | convolution fusion | flops 137363968 | bytes 4727808 | tf_op jit(solution)/shard_map/while/body/eval_jaxpr/sub | solution.py:44
  47.7 3.4 %fusion.152 = bf16[3,4,512,64]{2,3,1,0:T(8,128)(2,1)} fusion(bf16[3,4,512,64]{2,3,1,0:T(8,128)(2,1)} %get-tuple-element.177, s32[]{:T(128)S(6)} %copy.35, f32[4,512,512]{1,2,0:T(8,128)} %get-tuple-element.168, f32[4,512]{1,0:T(4,128)S(1)} %get-tuple-element.169, bf16[3,4,512,64]{2,3,1,0:T(8,128)(2,1)S(1)} %get-tuple-element.186), kind=kOutput, calls=%fused_computation.33.clone.1 | convolution fusion | flops 136314880 | bytes 4989952 | tf_op jit(solution)/shard_map/while/body/eval_jaxpr/hts,hsd->htd/dot_general | solution.py:46
  51.0 4.5 %fusion.151 = (f32[4,512]{1,0:T(4,128)S(1)}, f32[4,512,512]{1,2,0:T(8,128)}) fusion(bf16[3,4,512,64]{2,3,1,0:T(8,128)(2,1)} %get-tuple-element.185, s32[]{:T(128)S(6)} %copy.35, bf16[3,4,512,64]{2,3,1,0:T(8,128)(2,1)} %get-tuple-element.184), kind=kOutput, calls=%fused_computation.101.clone.1 | convolution fusion | flops 137363968 | bytes 4727808 | tf_op jit(solution)/shard_map/while/body/eval_jaxpr/sub | solution.py:44
  55.5 3.4 %fusion.152 = bf16[3,4,512,64]{2,3,1,0:T(8,128)(2,1)} fusion(bf16[3,4,512,64]{2,3,1,0:T(8,128)(2,1)} %get-tuple-element.177, s32[]{:T(128)S(6)} %copy.35, f32[4,512,512]{1,2,0:T(8,128)} %get-tuple-element.168, f32[4,512]{1,0:T(4,128)S(1)} %get-tuple-element.169, bf16[3,4,512,64]{2,3,1,0:T(8,128)(2,1)S(1)} %get-tuple-element.186), kind=kOutput, calls=%fused_computation.33.clone.1 | convolution fusion | flops 136314880 | bytes 4989952 | tf_op jit(solution)/shard_map/while/body/eval_jaxpr/hts,hsd->htd/dot_general | solution.py:46
  58.9 4.5 %fusion.151 = (f32[4,512]{1,0:T(4,128)S(1)}, f32[4,512,512]{1,2,0:T(8,128)}) fusion(bf16[3,4,512,64]{2,3,1,0:T(8,128)(2,1)} %get-tuple-element.185, s32[]{:T(128)S(6)} %copy.35, bf16[3,4,512,64]{2,3,1,0:T(8,128)(2,1)} %get-tuple-element.184), kind=kOutput, calls=%fused_computation.101.clone.1 | convolution fusion | flops 137363968 | bytes 4727808 | tf_op jit(solution)/shard_map/while/body/eval_jaxpr/sub | solution.py:44
  63.4 3.4 %fusion.152 = bf16[3,4,512,64]{2,3,1,0:T(8,128)(2,1)} fusion(bf16[3,4,512,64]{2,3,1,0:T(8,128)(2,1)} %get-tuple-element.177, s32[]{:T(128)S(6)} %copy.35, f32[4,512,512]{1,2,0:T(8,128)} %get-tuple-element.168, f32[4,512]{1,0:T(4,128)S(1)} %get-tuple-element.169, bf16[3,4,512,64]{2,3,1,0:T(8,128)(2,1)S(1)} %get-tuple-element.186), kind=kOutput, calls=%fused_computation.33.clone.1 | convolution fusion | flops 136314880 | bytes 4989952 | tf_op jit(solution)/shard_map/while/body/eval_jaxpr/hts,hsd->htd/dot_general | solution.py:46
  66.7 0.3 copy.23
  67.0 0.3 copy.22
  67.3 0.1 broadcast.75.clone.1
  67.4 18.4 %while.20 = (s32[]{:T(128)}, bf16[3,4,512,64]{2,3,1,0:T(8,128)(2,1)S(1)}, bf16[3,4,512,64]{2,3,1,0:T(8,128)(2,1)S(1)}, bf16[3,4,512,64]{2,3,1,0:T(8,128)(2,1)S(1...) while((s32[]{:T(128)}, bf16[3,4,512,64]{2,3,1,0:T(8,128)(2,1)S(1)}, bf16[3,4,512,64]{2,3,1,0:T(8,128)(2,1)S(1)}, ...), condition=%wide.region_3.4_spmd, body=%wide.region_0.3_spmd.sunk | while | flops 273678848 | bytes 9717837 | solution.py:48
  67.4 3.4 %fusion.146 = (f32[4,512]{1,0:T(4,128)S(1)}, f32[4,512,512]{1,2,0:T(8,128)}) fusion(bf16[3,4,512,64]{2,3,1,0:T(8,128)(2,1)S(1)} %get-tuple-element.203, s32[]{:T(128)S(6)} %copy.41, bf16[3,4,512,64]{2,3,1,0:T(8,128)(2,1)S(1)} %get-tuple-element.202), kind=kOutput, calls=%fused_computation.100.clone.1 | convolution fusion | flops 137363968 | bytes 4727808 | tf_op jit(solution)/shard_map/while/body/eval_jaxpr/sub | solution.py:44
  70.8 2.7 %fusion.147 = bf16[3,4,512,64]{2,3,1,0:T(8,128)(2,1)S(1)} fusion(bf16[3,4,512,64]{2,3,1,0:T(8,128)(2,1)S(1)} %get-tuple-element.195, s32[]{:T(128)S(6)} %copy.41, f32[4,512,512]{1,2,0:T(8,128)} %get-tuple-element.161, f32[4,512]{1,0:T(4,128)S(1)} %get-tuple-element.162, bf16[3,4,512,64]{2,3,1,0:T(8,128)(2,1)S(1)} %get-tuple-element.204), kind=kOutput, calls=%fused_computation.8.clone.1 | convolution fusion | flops 136314880 | bytes 4989952 | tf_op jit(solution)/shard_map/while/body/eval_jaxpr/hts,hsd->htd/dot_general | solution.py:46
  73.5 3.4 %fusion.146 = (f32[4,512]{1,0:T(4,128)S(1)}, f32[4,512,512]{1,2,0:T(8,128)}) fusion(bf16[3,4,512,64]{2,3,1,0:T(8,128)(2,1)S(1)} %get-tuple-element.203, s32[]{:T(128)S(6)} %copy.41, bf16[3,4,512,64]{2,3,1,0:T(8,128)(2,1)S(1)} %get-tuple-element.202), kind=kOutput, calls=%fused_computation.100.clone.1 | convolution fusion | flops 137363968 | bytes 4727808 | tf_op jit(solution)/shard_map/while/body/eval_jaxpr/sub | solution.py:44
  77.0 2.7 %fusion.147 = bf16[3,4,512,64]{2,3,1,0:T(8,128)(2,1)S(1)} fusion(bf16[3,4,512,64]{2,3,1,0:T(8,128)(2,1)S(1)} %get-tuple-element.195, s32[]{:T(128)S(6)} %copy.41, f32[4,512,512]{1,2,0:T(8,128)} %get-tuple-element.161, f32[4,512]{1,0:T(4,128)S(1)} %get-tuple-element.162, bf16[3,4,512,64]{2,3,1,0:T(8,128)(2,1)S(1)} %get-tuple-element.204), kind=kOutput, calls=%fused_computation.8.clone.1 | convolution fusion | flops 136314880 | bytes 4989952 | tf_op jit(solution)/shard_map/while/body/eval_jaxpr/hts,hsd->htd/dot_general | solution.py:46
  79.7 3.4 %fusion.146 = (f32[4,512]{1,0:T(4,128)S(1)}, f32[4,512,512]{1,2,0:T(8,128)}) fusion(bf16[3,4,512,64]{2,3,1,0:T(8,128)(2,1)S(1)} %get-tuple-element.203, s32[]{:T(128)S(6)} %copy.41, bf16[3,4,512,64]{2,3,1,0:T(8,128)(2,1)S(1)} %get-tuple-element.202), kind=kOutput, calls=%fused_computation.100.clone.1 | convolution fusion | flops 137363968 | bytes 4727808 | tf_op jit(solution)/shard_map/while/body/eval_jaxpr/sub | solution.py:44
  83.1 2.7 %fusion.147 = bf16[3,4,512,64]{2,3,1,0:T(8,128)(2,1)S(1)} fusion(bf16[3,4,512,64]{2,3,1,0:T(8,128)(2,1)S(1)} %get-tuple-element.195, s32[]{:T(128)S(6)} %copy.41, f32[4,512,512]{1,2,0:T(8,128)} %get-tuple-element.161, f32[4,512]{1,0:T(4,128)S(1)} %get-tuple-element.162, bf16[3,4,512,64]{2,3,1,0:T(8,128)(2,1)S(1)} %get-tuple-element.204), kind=kOutput, calls=%fused_computation.8.clone.1 | convolution fusion | flops 136314880 | bytes 4989952 | tf_op jit(solution)/shard_map/while/body/eval_jaxpr/hts,hsd->htd/dot_general | solution.py:46
  85.8 0.0 copy-start.2
  85.8 0.0 copy-start.6
  85.9 2.5 %fusion.112 = (f32[512]{0:T(512)S(1)}, f32[512,768]{1,0:T(8,128)S(1)}) fusion(bf16[512,768]{0,1:T(8,128)(2,1)S(1)} %bitcast.159, bf16[768,768]{1,0:T(8,128)(2,1)} %param.21, bf16[512,768]{1,0:T(8,128)(2,1)} %copy-done.10), kind=kOutput, calls=%fused_computation.105 | convolution fusion | flops 605158912 | bytes 4327424 | tf_op jit(solution)/shard_map/dot_general | solution.py:50
  88.4 0.3 multiply_reduce_fusion.3
  88.7 0.0 copy-start.7
  88.7 0.0 slice-start
  88.8 0.9 fusion.111
  89.7 0.3 multiply_reduce_fusion.2
  90.0 0.0 slice-start.1
  90.0 5.5 %convolution_multiply_fusion = f32[512,3456]{1,0:T(8,128)S(1)} fusion(bf16[768,3456]{1,0:T(8,128)(2,1)} %param.23, f32[512]{0:T(512)S(1)} %bitcast.163, f32[512,768]{1,0:T(8,128)S(1)} %get-tuple-element.95, f32[512]{0:T(512)S(1)} %add_sqrt_fusion, f32[512]{0:T(512)S(1)} %broadcast_multiply_fusion, f32[768]{0:T(1024)S(1)} %copy-done.7), kind=kOutput, calls=%fused_computation.58 | convolution fusion | flops 2721251328 | bytes 13968384 | tf_op jit(solution)/shard_map/dot_general | solution.py:54
  95.5 3.1 %convolution_multiply_fusion.1 = f32[512,3456]{1,0:T(8,128)S(1)} fusion(bf16[768,3456]{1,0:T(8,128)(2,1)S(1)} %bitcast.169, f32[512]{0:T(512)S(1)} %bitcast.161, f32[512,768]{1,0:T(8,128)S(1)} %get-tuple-element.97, f32[768]{0:T(1024)S(1)} %copy-done.7, f32[512]{0:T(512)S(1)} %add_sqrt_fusion.1, f32[512]{0:T(512)S(1)} %broadcast_multiply_fusion.1), kind=kOutput, calls=%fused_computation.59 | convolution fusion | flops 2721251328 | bytes 13968384 | tf_op jit(solution)/shard_map/dot_general | solution.py:54
  98.7 7.7 %multiply_add_fusion = f32[3,512,3456]{2,1,0:T(8,128)} fusion(f32[512,3456]{1,0:T(8,128)S(1)} %convolution_multiply_fusion, f32[3]{0:T(128)S(1)} %get-tuple-element.98, f32[512,3456]{1,0:T(8,128)S(1)} %convolution_multiply_fusion.1, f32[3]{0:T(128)S(1)} %get-tuple-element.99), kind=kLoop, calls=%fused_computation.50 | loop fusion | flops 15925248 | bytes 35389464 | tf_op jit(solution)/shard_map/add | solution.py:76
  106.4 10.9 %slice_bitcast_fusion.1 = (f32[512,3456]{1,0:T(8,128)}, f32[512,3456]{1,0:T(8,128)}) fusion(f32[3,512,3456]{2,1,0:T(8,128)} %multiply_add_fusion), kind=kLoop, calls=%fused_computation.52 | loop fusion | bytes 28311552 | tf_op jit(solution)/shard_map/squeeze | solution.py:80
  117.3 7.1 %collective-permute-start.2 = (f32[512,3456]{1,0:T(8,128)}, f32[512,3456]{1,0:T(8,128)S(1)}, u32[]{:S(2)}, u32[]{:S(2)}) collective-permute-start(f32[512,3456]{1,0:T(8,128)} %get-tuple-element.85), channel_id=1, source_target_pairs={{1,0},{2,1},{3,2},{4,3},{5,4},{6,5},{7,6},{8,7},{9,8},{10,9},{11,1... | collective-permute-start | bytes 21233672 | tf_op jit(solution)/shard_map/ppermute | solution.py:26
  124.4 1.9 collective-permute-start.3
  126.3 0.1 multiply_add_fusion.1
  126.4 1.9 collective-permute-start.5
  128.3 7.9 %collective-permute-start.4 = (f32[512]{0:T(512)S(1)}, f32[512]{0:T(512)S(1)}, u32[]{:S(2)}, u32[]{:S(2)}) collective-permute-start(f32[512]{0:T(512)S(1)} %bitcast.166), channel_id=1, source_target_pairs={{1,0},{2,1},{3,2},{4,3},{5,4},{6,5},{7,6},{8,7},{9,8},{10,9},{11,1... | collective-permute-start | bytes 6152 | tf_op jit(solution)/shard_map/ppermute | solution.py:26
  136.2 73.4 %collective-permute-done.5 = f32[512]{0:T(512)S(1)} collective-permute-done((f32[512]{0:T(512)S(1)}, f32[512]{0:T(512)S(1)}, u32[]{:S(2)}, u32[]{:S(2)}) %collective-permute-start.5) | collective-permute-done | bytes 2080 | tf_op jit(solution)/shard_map/ppermute | solution.py:26
  209.5 0.0 collective-permute-done.2
  209.6 0.0 copy-start.1
  209.6 5.1 %fusion.78 = bf16[1,512,3456]{2,1,0:T(8,128)(2,1)} fusion(f32[512]{0:T(512)S(1)} %add_maximum_fusion, f32[512,3456]{1,0:T(8,128)S(1)} %collective-permute-done.3, f32[512,3456]{1,0:T(8,128)S(1)} %collective-permute-done.2, f32[3,512,3456]{2,1,0:T(8,128)} %multiply_add_fusion), kind=kLoop, calls=%fused_computation.60 | loop fusion | flops 7077888 | bytes 24774656 | tf_op jit(solution)/shard_map/broadcast_in_dim | solution.py:84
  (27 shorter events, 0.1 us)
Async XLA Ops:
  0.0 25.2 %copy-start = (bf16[1024,768]{1,0:T(8,128)(2,1)S(1)}, bf16[1024,768]{1,0:T(8,128)(2,1)}, u32[]{:S(2)}) copy-start(bf16[1024,768]{1,0:T(8,128)(2,1)} %param.17) | copy-start | bytes 4718596
  0.0 22.5 %collective-permute-start = (bf16[1,512,1024]{2,1,0:T(8,128)(2,1)}, bf16[1,512,1024]{2,1,0:T(8,128)(2,1)}, u32[]{:S(2)}, u32[]{:S(2)}) collective-permute-start(bf16[1,512,1024]{2,1,0:T(8,128)(2,1)} %param.14), channel_id=1, source_target_pairs={{0,1},{1,2},{2,3},{3,4},{4,5},{5,6},{6,7},{7,8},{8,9},{9,10},{10,1... | collective-permute-start | bytes 3145736 | tf_op jit(solution)/shard_map/ppermute | solution.py:15
  2.1 23.0 %collective-permute-start.1 = (bf16[1,512,1024]{2,1,0:T(8,128)(2,1)}, bf16[1,512,1024]{2,1,0:T(8,128)(2,1)S(1)}, u32[]{:S(2)}, u32[]{:S(2)}) collective-permute-start(bf16[1,512,1024]{2,1,0:T(8,128)(2,1)} %param.14), channel_id=1, source_target_pairs={{1,0},{2,1},{3,2},{4,3},{5,4},{6,5},{7,6},{8,7},{9,8},{10,9},{11,1... | collective-permute-start | bytes 3145736 | tf_op jit(solution)/shard_map/ppermute | solution.py:18
  26.2 9.0 %copy-start.8 = (bf16[512,768]{1,0:T(8,128)(2,1)}, bf16[512,768]{1,0:T(8,128)(2,1)S(1)}, u32[]{:S(2)}) copy-start(bf16[512,768]{1,0:T(8,128)(2,1)S(1)} %convolution_convert_fusion.6) | copy-start | bytes 2359300
  26.2 1.6 copy-start.4
  27.7 5.7 %copy-start.10 = (bf16[512,768]{1,0:T(8,128)(2,1)}, bf16[512,768]{1,0:T(8,128)(2,1)S(1)}, u32[]{:S(2)}) copy-start(bf16[512,768]{1,0:T(8,128)(2,1)S(1)} %convolution_convert_fusion.7) | copy-start | bytes 2359300
  27.7 1.6 copy-start.3
  31.0 2.5 %copy-start.5 = (bf16[768,768]{1,0:T(8,128)(2,1)S(1)}, bf16[768,768]{1,0:T(8,128)(2,1)}, u32[]{:S(2)}) copy-start(bf16[768,768]{1,0:T(8,128)(2,1)} %param.19) | copy-start | bytes 3538948
  85.8 2.9 %copy-start.2 = (bf16[3,4,512,64]{2,3,1,0:T(8,128)(2,1)S(1)}, bf16[3,4,512,64]{2,3,1,0:T(8,128)(2,1)}, u32[]{:S(2)}) copy-start(bf16[3,4,512,64]{2,3,1,0:T(8,128)(2,1)} %get-tuple-element.60) | copy-start | bytes 2359300
  85.8 2.9 %copy-start.6 = (bf16[768,768]{1,0:T(8,128)(2,1)S(1)}, bf16[768,768]{1,0:T(8,128)(2,1)}, u32[]{:S(2)}) copy-start(bf16[768,768]{1,0:T(8,128)(2,1)} %param.21) | copy-start | bytes 3538948
  85.8 2.9 %copy-start.9 = (bf16[512,768]{1,0:T(8,128)(2,1)S(1)}, bf16[512,768]{1,0:T(8,128)(2,1)}, u32[]{:S(2)}) copy-start(bf16[512,768]{1,0:T(8,128)(2,1)} %copy-done.8) | copy-start | bytes 2359300
  88.7 1.3 copy-start.7
  88.7 6.8 %slice-start = ((s8[5308416]{0:T(1024)(128)(4,1)}), s8[4194304]{0:T(1024)(128)(4,1)S(1)}, s32[]{:S(2)}) async-start(s8[5308416]{0:T(1024)(128)(4,1)} %bitcast.168), calls=%async_computation | async-start | bytes 8388608
  90.0 5.5 %slice-start.1 = ((s8[5308416]{0:T(1024)(128)(4,1)}), s8[1114112]{0:T(1024)(128)(4,1)S(1)}, s32[]{:S(2)}) async-start(s8[5308416]{0:T(1024)(128)(4,1)} %bitcast.168), calls=%async_computation.1 | async-start | bytes 2228224
  117.3 92.3 %collective-permute-start.2 = (f32[512,3456]{1,0:T(8,128)}, f32[512,3456]{1,0:T(8,128)S(1)}, u32[]{:S(2)}, u32[]{:S(2)}) collective-permute-start(f32[512,3456]{1,0:T(8,128)} %get-tuple-element.85), channel_id=1, source_target_pairs={{1,0},{2,1},{3,2},{4,3},{5,4},{6,5},{7,6},{8,7},{9,8},{10,9},{11,1... | collective-permute-start | bytes 21233672 | tf_op jit(solution)/shard_map/ppermute | solution.py:26
  124.4 85.2 %collective-permute-start.3 = (f32[512,3456]{1,0:T(8,128)}, f32[512,3456]{1,0:T(8,128)S(1)}, u32[]{:S(2)}, u32[]{:S(2)}) collective-permute-start(f32[512,3456]{1,0:T(8,128)} %get-tuple-element.86), channel_id=1, source_target_pairs={{0,1},{1,2},{2,3},{3,4},{4,5},{5,6},{6,7},{7,8},{8,9},{9,10},{10,1... | collective-permute-start | bytes 21233672 | tf_op jit(solution)/shard_map/ppermute | solution.py:26
  126.4 83.2 %collective-permute-start.5 = (f32[512]{0:T(512)S(1)}, f32[512]{0:T(512)S(1)}, u32[]{:S(2)}, u32[]{:S(2)}) collective-permute-start(f32[512]{0:T(512)S(1)} %bitcast.167), channel_id=1, source_target_pairs={{0,1},{1,2},{2,3},{3,4},{4,5},{5,6},{6,7},{7,8},{8,9},{9,10},{10,1... | collective-permute-start | bytes 6152 | tf_op jit(solution)/shard_map/ppermute | solution.py:26
  128.3 81.2 %collective-permute-start.4 = (f32[512]{0:T(512)S(1)}, f32[512]{0:T(512)S(1)}, u32[]{:S(2)}, u32[]{:S(2)}) collective-permute-start(f32[512]{0:T(512)S(1)} %bitcast.166), channel_id=1, source_target_pairs={{1,0},{2,1},{3,2},{4,3},{5,4},{6,5},{7,6},{8,7},{9,8},{10,9},{11,1... | collective-permute-start | bytes 6152 | tf_op jit(solution)/shard_map/ppermute | solution.py:26
  209.6 5.1 %copy-start.1 = (bf16[1024,768]{1,0:T(8,128)(2,1)S(1)}, bf16[1024,768]{1,0:T(8,128)(2,1)}, u32[]{:S(2)}) copy-start(bf16[1024,768]{1,0:T(8,128)(2,1)} %param.17) | copy-start | bytes 4718596
where the time goes:
time: 216 us; the launch traced here: 215 us
  waiting for transfers between devices  80.8 us (37%)
  matrix products  63.3 us (29%)
  starting transfers between devices  30.4 us (14%)
  local copies, waits for them, and re-layouts  24.2 us (11%)
  other arithmetic  14.3 us (7%)
    ppermute x4, waiting for transfers between devices, passed_along(): return lax.ppermute(block, axis, route)  73.4 us
    sub x6, matrix products, attend(): expo = jnp.exp(scores - top)  23.8 us
    ppermute x4, starting transfers between devices, passed_along(): return lax.ppermute(block, axis, route)  18.8 us
    dot_general x6, matrix products, attend(): jnp.einsum('hts,hsd->htd', probs, vb, preferred_element_type=jnp.float32)  18.2 us
    squeeze x1, local copies, waits for them, and re-layouts, on_device(): from_upper = passed_along((terms[0], sums[0]), ('group', 'dev'), -1)  10.9 us
    ppermute x1, starting transfers between devices, extended(): lax.ppermute(lax.slice_in_dim(block, 0, width, axis=dim), axis, backward)  9.58 us
    dot_general x2, matrix products, cross_branch(): return jnp.dot(normed, w_head, preferred_element_type=jnp.float32)  8.62 us
    add x1, other arithmetic, on_device(): pick_a[:, None, None] * (conf_a[:, None] * out_a)[None]  7.69 us
  transfers between devices with their start and end apart: 6, of which 2 were waited for; matrix products, arithmetic and copies ran while one was open for 2% of the time, Pallas kernels for 0%

commit v1 on v0

v1 whole, which is shorter than its diff:
```python
import functools

import jax
import jax.numpy as jnp
from jax import lax
from jax.experimental import pallas as pl
from jax.experimental.pallas import tpu as pltpu
from jax.sharding import PartitionSpec as P

HEADS = 12
HEAD_DIM = 64
PAIRED = 2 * HEAD_DIM
LOG2E = 1.4426950408889634
MESH = pl.DeviceIdType.MESH
BF16 = jnp.bfloat16
F32 = jnp.float32
SEND_ROWS = 128
ROWS = 128


def dot(a, b):
    return jnp.dot(a, b, preferred_element_type=F32)


def kernel(
    mesh_shape,
    pair_ref,
    conf_ref,
    gain_ref,
    tokens_hbm,
    w_embed_hbm,
    w_query_hbm,
    w_key_hbm,
    w_value_hbm,
    w_out_hbm,
    merged_ref,
    tokens,
    w_embed,
    w_query,
    w_key,
    w_value,
    w_out,
    own,
    from_fast,
    from_slow,
    x_u,
    q_even,
    q_odd,
    k_u,
    k_w,
    v_even_u,
    v_odd_u,
    v_even_w,
    v_odd_w,
    context,
    normed_u,
    normed_w,
    back_fast,
    back_slow,
    conf_out,
    conf_fast,
    conf_slow,
    load_sem,
    send_sem,
    recv_fast_sem,
    recv_slow_sem,
    send_back_sem,
    recv_back_fast_sem,
    recv_back_slow_sem,
    conf_sem,
):
    n_group, n_dev = mesh_shape
    n = n_group * n_dev
    me = lax.axis_index("group") * n_dev + lax.axis_index("dev")
    odd = lax.rem(me, 2)
    fast = me + 1 - 2 * odd
    slow = lax.rem(me + 2 * odd - 1 + n, n)
    fast_id = (lax.div(fast, n_dev), lax.rem(fast, n_dev))
    slow_id = (lax.div(slow, n_dev), lax.rem(slow, n_dev))

    loads = [
        pltpu.make_async_copy(src, dst, load_sem.at[i])
        for i, (src, dst) in enumerate(
            (
                (tokens_hbm, tokens),
                (w_embed_hbm, w_embed),
                (w_key_hbm, w_key),
                (w_value_hbm, w_value),
                (w_query_hbm, w_query),
                (w_out_hbm, w_out),
            )
        )
    ]
    for load in loads:
        load.start()

    barrier = pltpu.get_barrier_semaphore()
    pl.semaphore_signal(barrier, inc=1, device_id=fast_id, device_id_type=MESH)
    pl.semaphore_signal(barrier, inc=1, device_id=slow_id, device_id_type=MESH)

    first, second = pair_ref[0, 0], pair_ref[0, 1]
    has_fast = jnp.logical_or(first == fast, second == fast)
    has_slow = jnp.logical_or(first == slow, second == slow)
    u_image = jnp.where(has_fast, fast, me)
    u_first = (first == u_image).astype(F32)
    f_fast, f_slow = has_fast.astype(F32), has_slow.astype(F32)
    conf_first = conf_ref[0, 0:1, :].astype(F32)
    conf_second = conf_ref[0, 1:2, :].astype(F32)
    conf_u = conf_first * u_first + conf_second * (1.0 - u_first)
    conf_w = conf_second * u_first + conf_first * (1.0 - u_first)
    conf_out[...] = jnp.concatenate(
        [
            conf_u * f_fast,
            conf_w * f_slow,
            conf_u * (1.0 - f_fast),
            conf_w * (1.0 - f_slow),
            jnp.zeros((4, conf_u.shape[1]), F32),
        ],
        axis=0,
    )
    pl.semaphore_wait(barrier, 2)

    def remote(src, dst, send, recv, target):
        return pltpu.make_async_remote_copy(
            src_ref=src,
            dst_ref=dst,
            send_sem=send,
            recv_sem=recv,
            device_id=target,
            device_id_type=MESH,
        )

    def rows_of(step, size):
        return pl.ds(pl.multiple_of(step * size, size), size)

    tok = own.shape[0]
    sends = tok // SEND_ROWS
    steps = tok // ROWS

    def to_fast(i):
        block = rows_of(i, SEND_ROWS)
        return remote(own.at[block], from_fast.at[block], send_sem.at[0, i], recv_fast_sem.at[i], fast_id)

    def to_slow(i):
        block = rows_of(i, SEND_ROWS)
        return remote(own.at[block], from_slow.at[block], send_sem.at[1, i], recv_slow_sem.at[i], slow_id)

    def conf_copies():
        return (
            remote(conf_out, conf_fast, conf_sem.at[0], conf_sem.at[1], fast_id),
            remote(conf_out, conf_slow, conf_sem.at[2], conf_sem.at[3], slow_id),
        )

    loads[0].wait()
    loads[1].wait()

    def embed(i, carry):
        block = rows_of(i, SEND_ROWS)
        own[block, :] = dot(tokens[0, block, :], w_embed[...]).astype(BF16)
        to_slow(i).start()
        to_fast(i).start()
        return carry

    lax.fori_loop(0, sends, embed, 0)
    for copy in conf_copies():
        copy.start()

    lower_half = lax.broadcasted_iota(jnp.int32, (1, HEADS * HEAD_DIM), 1) % PAIRED < HEAD_DIM

    def put_query(block, x):
        q = dot(x, w_query[...]) * (LOG2E / HEAD_DIM**0.5)
        q_even[block, :] = jnp.where(lower_half, q, 0.0).astype(BF16)
        q_odd[block, :] = jnp.where(lower_half, 0.0, q).astype(BF16)

    def put_key_value(block, x, k_ref, v_even_ref, v_odd_ref):
        k_ref[block, :] = dot(x, w_key[...]).astype(BF16)
        v = dot(x, w_value[...])
        v_even_ref[block, :] = jnp.where(lower_half, v, 1.0).astype(BF16)
        v_odd_ref[block, :] = jnp.where(lower_half, 1.0, v).astype(BF16)

    half = lax.broadcasted_iota(jnp.int32, (1, PAIRED), 1) < HEAD_DIM

    def attend(block, x, k_ref, v_even_ref, v_odd_ref):
        for j in range(HEADS // 2):
            lanes = slice(j * PAIRED, (j + 1) * PAIRED)
            k = k_ref[:, lanes]
            both = []
            for q_ref, v_ref in ((q_even, v_even_ref), (q_odd, v_odd_ref)):
                scores = lax.dot_general(
                    q_ref[block, lanes], k, (((1,), (1,)), ((), ())), preferred_element_type=F32
                )
                top = jnp.max(scores, axis=1, keepdims=True)
                expo = jnp.exp2(scores - top).astype(BF16)
                both.append(dot(expo, v_ref[:, lanes]))
            even, odd_ = both
            total = jnp.where(half, even, odd_)
            weight = pltpu.roll(jnp.where(half, odd_, even), HEAD_DIM, 1)
            context[block, lanes] = (total / weight).astype(BF16)
        mixed = x.astype(F32) + dot(context[block, :], w_out[...])
        center = mixed - jnp.mean(mixed, axis=-1, keepdims=True)
        spread = jnp.mean(center * center, axis=-1, keepdims=True)
        return (center * lax.rsqrt(spread + 1e-06) * gain_ref[...]).astype(BF16)

    for load in loads[2:]:
        load.wait()

    def take_u(i, carry):
        to_fast(i).wait_recv()
        block = rows_of(i, SEND_ROWS)
        x = jnp.where(has_fast, from_fast[block, :], own[block, :])
        x_u[block, :] = x
        put_key_value(block, x, k_u, v_even_u, v_odd_u)
        return carry

    lax.fori_loop(0, sends, take_u, 0)

    def back_copy(i, of_u):
        block = rows_of(i, ROWS)
        if of_u:
            return remote(normed_u.at[block], back_fast.at[block], send_back_sem.at[0, i], recv_back_fast_sem.at[i], fast_id)
        return remote(normed_w.at[block], back_slow.at[block], send_back_sem.at[1, i], recv_back_slow_sem.at[i], slow_id)

    def branch_w(i, carry):
        to_slow(i).wait_recv()
        block = rows_of(i, ROWS)
        x = jnp.where(has_slow, from_slow[block, :], own[block, :])
        put_query(block, x)
        put_key_value(block, x, k_w, v_even_w, v_odd_w)
        normed_w[block, :] = attend(block, x, k_u, v_even_u, v_odd_u)
        back_copy(i, False).start()
        return carry

    lax.fori_loop(0, steps, branch_w, 0)

    def branch_u(i, carry):
        block = rows_of(i, ROWS)
        x = x_u[block, :]
        put_query(block, x)
        normed_u[block, :] = attend(block, x, k_w, v_even_w, v_odd_w)
        back_copy(i, True).start()
        return carry

    lax.fori_loop(0, steps, branch_u, 0)

    for copy in conf_copies():
        copy.wait()
    parts = jnp.concatenate(
        [conf_fast[0:1, :], conf_slow[1:2, :], conf_out[2:4, :], jnp.zeros((4, tok), F32)], axis=0
    )
    weight = jnp.sum(parts, axis=0, keepdims=True)
    shares = jnp.transpose(parts / jnp.maximum(weight, 1.0))

    for i in range(steps):
        block = rows_of(i, ROWS)
        back_copy(i, True).wait_recv()
        back_copy(i, False).wait_recv()
        s = shares[i * ROWS : (i + 1) * ROWS, :]
        merged = s[:, 0:1] * back_fast[block, :].astype(F32)
        merged += s[:, 1:2] * back_slow[block, :].astype(F32)
        merged += s[:, 2:3] * normed_u[block, :].astype(F32)
        merged += s[:, 3:4] * normed_w[block, :].astype(F32)
        merged_ref[block, :] = merged.astype(BF16)

    for i in range(sends):
        to_fast(i).wait_send()
        to_slow(i).wait_send()
    for i in range(steps):
        back_copy(i, True).wait_send()
        back_copy(i, False).wait_send()


def merged_normed(mesh_shape, pair_list, confidence, tokens, w_embed, w_query, w_key, w_value, w_out, norm_gain):
    tok = tokens.shape[1]
    width = w_embed.shape[1]
    any_space = pl.BlockSpec(memory_space=pl.ANY)
    vmem = pl.BlockSpec(memory_space=pltpu.VMEM)
    rows = pltpu.VMEM((tok, width), BF16)
    return pl.pallas_call(
        functools.partial(kernel, mesh_shape),
        out_shape=jax.ShapeDtypeStruct((tok, width), BF16),
        in_specs=[pl.BlockSpec(memory_space=pltpu.SMEM), vmem, vmem] + [any_space] * 6,
        out_specs=vmem,
        scratch_shapes=[
            pltpu.VMEM(tokens.shape, BF16),
            pltpu.VMEM(w_embed.shape, BF16),
            pltpu.VMEM(w_query.shape, BF16),
            pltpu.VMEM(w_key.shape, BF16),
            pltpu.VMEM(w_value.shape, BF16),
            pltpu.VMEM(w_out.shape, BF16),
        ]
        + [rows] * 17
        + [pltpu.VMEM((8, tok), F32)] * 3
        + [
            pltpu.SemaphoreType.DMA((6,)),
            pltpu.SemaphoreType.DMA((2, tok // SEND_ROWS)),
            pltpu.SemaphoreType.DMA((tok // SEND_ROWS,)),
            pltpu.SemaphoreType.DMA((tok // SEND_ROWS,)),
            pltpu.SemaphoreType.DMA((2, tok // ROWS)),
            pltpu.SemaphoreType.DMA((tok // ROWS,)),
            pltpu.SemaphoreType.DMA((tok // ROWS,)),
            pltpu.SemaphoreType.DMA((4,)),
        ],
        compiler_params=pltpu.CompilerParams(
            collective_id=0, has_side_effects=True, vmem_limit_bytes=44 * 2**20
        ),
        name="pair_attention",
    )(pair_list, confidence, norm_gain[None], tokens, w_embed, w_query, w_key, w_value, w_out)


def solution(mesh):
    mesh_shape = (mesh.shape["group"], mesh.shape["dev"])

    def on_device(
        tokens, pair_list, confidence, w_embed, w_query, w_key, w_value, w_out, norm_gain, w_head
    ):
        merged = merged_normed(
            mesh_shape, pair_list, confidence, tokens, w_embed, w_query, w_key, w_value, w_out, norm_gain
        )
        return dot(merged, w_head).astype(BF16)[None]

    along = ("group", "dev")
    in_specs = (P(along, None, None), P(along, None), P(along, None, None)) + (P(),) * 7
    return jax.shard_map(
        on_device, mesh=mesh, in_specs=in_specs, out_specs=P(along, None, None), check_vma=False
    )
```

time: 216 us -> 66.5 us (0.31)
  the two profiles are of different devices: /device:TPU:24 before, /device:TPU:1 now
where the time goes in v1:
time: 66.5 us; the launch traced here: 66.2 us
  Pallas kernels  52 us (78%)
  local copies, waits for them, and re-layouts  9.75 us (15%)
  matrix products  4.42 us (7%)
    pallas_call x1, Pallas kernels, merged_normed(): pl.pallas_call(functools.partial(kernel, mesh_shape), out_shape=jax.Shape...  52 us
    unnamed x18, local copies, waits for them, and re-layouts  9.06 us
    dot_general x1, matrix products, dot(): return jnp.dot(a, b, preferred_element_type=F32)  4.42 us

profile of v1, /device:TPU:1, one launch (start us, length us, event | category | flops | bytes accessed | tf_op | source)
XLA Modules:
  0.0 66.2 jit_solution(12565884269653973508)
XLA Ops:
  0.0 0.7 %broadcast_in_dim.6.gain_ref = f32[1,768]{1,0:T(1,128)S(1)} reshape(f32[768]{0:T(1024)} %param.18) | data formatting | bytes 6144 | tf_op jit(solution)/shard_map/broadcast_in_dim | solution.py:307
  0.7 0.0 copy-start
  0.7 1.4 %copy-done = bf16[1024,768]{1,0:T(8,128)(2,1)S(1)} copy-done((bf16[1024,768]{1,0:T(8,128)(2,1)S(1)}, bf16[1024,768]{1,0:T(8,128)(2,1)}, u32[]{:S(2)}) %copy-start) | copy-done | bytes 1572888
  2.1 0.0 copy-start.1
  2.1 1.3 %copy-done.1 = bf16[768,768]{1,0:T(8,128)(2,1)S(1)} copy-done((bf16[768,768]{1,0:T(8,128)(2,1)S(1)}, bf16[768,768]{1,0:T(8,128)(2,1)}, u32[]{:S(2)}) %copy-start.1) | copy-done | bytes 1179672
  3.4 0.0 copy-start.2
  3.4 1.3 %copy-done.2 = bf16[768,768]{1,0:T(8,128)(2,1)S(1)} copy-done((bf16[768,768]{1,0:T(8,128)(2,1)S(1)}, bf16[768,768]{1,0:T(8,128)(2,1)}, u32[]{:S(2)}) %copy-start.2) | copy-done | bytes 1179672
  4.6 0.0 copy-start.3
  4.6 1.3 %copy-done.3 = bf16[768,768]{1,0:T(8,128)(2,1)S(1)} copy-done((bf16[768,768]{1,0:T(8,128)(2,1)S(1)}, bf16[768,768]{1,0:T(8,128)(2,1)}, u32[]{:S(2)}) %copy-start.3) | copy-done | bytes 1179672
  5.9 0.0 copy-start.4
  5.9 1.3 %copy-done.4 = bf16[768,768]{1,0:T(8,128)(2,1)S(1)} copy-done((bf16[768,768]{1,0:T(8,128)(2,1)S(1)}, bf16[768,768]{1,0:T(8,128)(2,1)}, u32[]{:S(2)}) %copy-start.4) | copy-done | bytes 1179672
  7.2 0.0 copy-start.5
  7.2 1.2 %copy-done.5 = bf16[1,512,1024]{2,1,0:T(8,128)(2,1)S(1)} copy-done((bf16[1,512,1024]{2,1,0:T(8,128)(2,1)S(1)}, bf16[1,512,1024]{2,1,0:T(8,128)(2,1)}, u32[]{:S(2)}) %copy-start.5) | copy-done | bytes 1048600
  8.4 0.0 copy-start.6
  8.4 0.7 %copy-done.6 = s32[1,2,512]{2,1,0:T(2,128)S(1)} copy-done((s32[1,2,512]{2,1,0:T(2,128)S(1)}, s32[1,2,512]{2,1,0:T(2,128)}, u32[]{:S(2)}) %copy-start.6) | copy-done | bytes 4120
  9.1 0.0 copy-start.7
  9.1 0.7 copy-done.7
  9.8 0.0 copy-start.8
  9.8 52.0 %pair_attention.1 = bf16[512,768]{1,0:T(8,128)(2,1)S(1)} custom-call(s32[1,2]{1,0:T(1,128)S(1)} %copy-done.7, s32[1,2,512]{2,1,0:T(2,128)S(1)} %copy-done.6, f32[1,768]{1,0:T(1,128)S(1)} %broadcast_in_dim.6.gain_ref, bf16[1,512,1024]{2,1,0:T(8,128)(2,1)S(1)} %copy-done.5, bf16[1024,768]{1,0:T(8,128)(2,1)S(1)} %copy-done, bf16[768,768]{1,0:T(8,128)(2,1)S(1)} %copy-done.1, ...), custom_call_target="tpu_custom_call" | custom-call | tf_op jit(solution)/shard_map/pair_attention/pallas_call | solution.py:278
  61.8 0.0 copy-done.8
  61.8 4.4 %fusion = bf16[1,512,3456]{2,1,0:T(8,128)(2,1)} fusion(bf16[512,768]{1,0:T(8,128)(2,1)S(1)} %pair_attention.1, bf16[768,3456]{1,0:T(8,128)(2,1)S(1)} %copy-done.8), kind=kOutput, calls=%fused_computation.1 | convolution fusion | flops 2719678464 | bytes 9633792 | tf_op jit(solution)/shard_map/dot_general | solution.py:22
Async XLA Ops:
  0.7 1.4 %copy-start = (bf16[1024,768]{1,0:T(8,128)(2,1)S(1)}, bf16[1024,768]{1,0:T(8,128)(2,1)}, u32[]{:S(2)}) copy-start(bf16[1024,768]{1,0:T(8,128)(2,1)} %w_embed_hbm.1) | copy-start | bytes 4718596
  2.1 1.3 %copy-start.1 = (bf16[768,768]{1,0:T(8,128)(2,1)S(1)}, bf16[768,768]{1,0:T(8,128)(2,1)}, u32[]{:S(2)}) copy-start(bf16[768,768]{1,0:T(8,128)(2,1)} %w_query_hbm.1) | copy-start | bytes 3538948
  3.4 1.3 %copy-start.2 = (bf16[768,768]{1,0:T(8,128)(2,1)S(1)}, bf16[768,768]{1,0:T(8,128)(2,1)}, u32[]{:S(2)}) copy-start(bf16[768,768]{1,0:T(8,128)(2,1)} %w_key_hbm.1) | copy-start | bytes 3538948
  4.6 1.3 %copy-start.3 = (bf16[768,768]{1,0:T(8,128)(2,1)S(1)}, bf16[768,768]{1,0:T(8,128)(2,1)}, u32[]{:S(2)}) copy-start(bf16[768,768]{1,0:T(8,128)(2,1)} %w_value_hbm.1) | copy-start | bytes 3538948
  5.9 1.3 %copy-start.4 = (bf16[768,768]{1,0:T(8,128)(2,1)S(1)}, bf16[768,768]{1,0:T(8,128)(2,1)}, u32[]{:S(2)}) copy-start(bf16[768,768]{1,0:T(8,128)(2,1)} %w_out_hbm.1) | copy-start | bytes 3538948
  7.2 1.2 %copy-start.5 = (bf16[1,512,1024]{2,1,0:T(8,128)(2,1)S(1)}, bf16[1,512,1024]{2,1,0:T(8,128)(2,1)}, u32[]{:S(2)}) copy-start(bf16[1,512,1024]{2,1,0:T(8,128)(2,1)} %tokens_hbm.1) | copy-start | bytes 3145732
  8.4 0.7 %copy-start.6 = (s32[1,2,512]{2,1,0:T(2,128)S(1)}, s32[1,2,512]{2,1,0:T(2,128)}, u32[]{:S(2)}) copy-start(s32[1,2,512]{2,1,0:T(2,128)} %conf_ref.1) | copy-start | bytes 12292
  9.1 0.7 copy-start.7
  9.8 52.0 %copy-start.8 = (bf16[768,3456]{1,0:T(8,128)(2,1)S(1)}, bf16[768,3456]{1,0:T(8,128)(2,1)}, u32[]{:S(2)}) copy-start(bf16[768,3456]{1,0:T(8,128)(2,1)} %param.19) | copy-start | bytes 15925252

commit v2 on v1

v2 whole, which is shorter than its diff:
```python
import functools

import jax
import jax.numpy as jnp
from jax import lax
from jax.experimental import pallas as pl
from jax.experimental.pallas import tpu as pltpu
from jax.sharding import PartitionSpec as P

HEADS = 12
HEAD_DIM = 64
PAIRED = 2 * HEAD_DIM
LOG2E = 1.4426950408889634
MESH = pl.DeviceIdType.MESH
BF16 = jnp.bfloat16
F32 = jnp.float32
SEND_ROWS = 128
ROWS = 256
AHEAD = 2


def dot(a, b):
    return jnp.dot(a, b, preferred_element_type=F32)


def kernel(
    mesh_shape,
    pair_hbm,
    conf_hbm,
    gain_hbm,
    tokens_hbm,
    w_embed_hbm,
    w_query_hbm,
    w_key_hbm,
    w_value_hbm,
    w_out_hbm,
    merged_ref,
    pair_ref,
    conf_ref,
    gain_ref,
    tokens,
    w_embed,
    w_query,
    w_key,
    w_value,
    w_out,
    own,
    from_fast,
    from_slow,
    x_u,
    q_even_u,
    q_odd_u,
    q_even_w,
    q_odd_w,
    k_u,
    k_w,
    v_even_u,
    v_odd_u,
    v_even_w,
    v_odd_w,
    context,
    normed_u,
    normed_w,
    back_fast,
    back_slow,
    conf_out,
    conf_fast,
    conf_slow,
    load_sem,
    send_sem,
    recv_fast_sem,
    recv_slow_sem,
    send_back_sem,
    recv_back_fast_sem,
    recv_back_slow_sem,
    conf_sem,
):
    n_group, n_dev = mesh_shape
    n = n_group * n_dev
    me = lax.axis_index("group") * n_dev + lax.axis_index("dev")
    odd = lax.rem(me, 2)
    fast = me + 1 - 2 * odd
    slow = lax.rem(me + 2 * odd - 1 + n, n)
    fast_id = (lax.div(fast, n_dev), lax.rem(fast, n_dev))
    slow_id = (lax.div(slow, n_dev), lax.rem(slow, n_dev))
    tok = own.shape[0]
    sends = tok // SEND_ROWS
    steps = tok // ROWS

    def rows_of(step, size):
        return pl.ds(step * size, size)

    loads = [
        pltpu.make_async_copy(src, dst, load_sem.at[i])
        for i, (src, dst) in enumerate(
            (
                (w_embed_hbm, w_embed),
                (tokens_hbm.at[0], tokens),
                (pair_hbm, pair_ref),
                (conf_hbm, conf_ref),
                (gain_hbm, gain_ref),
                (w_key_hbm, w_key),
                (w_value_hbm, w_value),
                (w_query_hbm, w_query),
                (w_out_hbm, w_out),
            )
        )
    ]
    for load in loads[:5]:
        load.start()

    barrier = pltpu.get_barrier_semaphore()
    pl.semaphore_signal(barrier, inc=1, device_id=fast_id, device_id_type=MESH)
    pl.semaphore_signal(barrier, inc=1, device_id=slow_id, device_id_type=MESH)

    def remote(src, dst, send, recv, target):
        return pltpu.make_async_remote_copy(
            src_ref=src,
            dst_ref=dst,
            send_sem=send,
            recv_sem=recv,
            device_id=target,
            device_id_type=MESH,
        )

    def to_fast(i):
        block = rows_of(i, SEND_ROWS)
        return remote(own.at[block], from_fast.at[block], send_sem.at[0, i], recv_fast_sem.at[i], fast_id)

    def to_slow(i):
        block = rows_of(i, SEND_ROWS)
        return remote(own.at[block], from_slow.at[block], send_sem.at[1, i], recv_slow_sem.at[i], slow_id)

    def conf_copies():
        return (
            remote(conf_out, conf_fast, conf_sem.at[0], conf_sem.at[1], fast_id),
            remote(conf_out, conf_slow, conf_sem.at[2], conf_sem.at[3], slow_id),
        )

    for load in loads[:2]:
        load.wait()
    for load in loads[5:]:
        load.start()
    for begin, end in ((0, SEND_ROWS), (SEND_ROWS, tok)):
        own[begin:end, :] = dot(tokens[begin:end, :], w_embed[...]).astype(BF16)
        if begin == 0:
            pl.semaphore_wait(barrier, 2)
        for i in range(begin // SEND_ROWS, end // SEND_ROWS):
            to_slow(i).start()
        for i in range(begin // SEND_ROWS, end // SEND_ROWS):
            to_fast(i).start()

    for load in loads[2:5]:
        load.wait()
    first, second = pair_ref[0, 0], pair_ref[0, 1]
    has_fast = jnp.logical_or(first == fast, second == fast)
    has_slow = jnp.logical_or(first == slow, second == slow)
    u_image = jnp.where(has_fast, fast, me)
    u_first = (first == u_image).astype(F32)
    f_fast, f_slow = has_fast.astype(F32), has_slow.astype(F32)
    conf_first = conf_ref[0, 0:1, :].astype(F32)
    conf_second = conf_ref[0, 1:2, :].astype(F32)
    conf_u = conf_first * u_first + conf_second * (1.0 - u_first)
    conf_w = conf_second * u_first + conf_first * (1.0 - u_first)
    conf_out[...] = jnp.concatenate(
        [
            conf_u * f_fast,
            conf_w * f_slow,
            conf_u * (1.0 - f_fast),
            conf_w * (1.0 - f_slow),
            jnp.zeros((4, tok), F32),
        ],
        axis=0,
    )
    for copy in conf_copies():
        copy.start()

    lower_half = lax.broadcasted_iota(jnp.int32, (1, HEADS * HEAD_DIM), 1) % PAIRED < HEAD_DIM
    half = lax.broadcasted_iota(jnp.int32, (1, PAIRED), 1) < HEAD_DIM

    def put_query(block, x, even_ref, odd_ref):
        q = dot(x, w_query[...]) * (LOG2E / HEAD_DIM**0.5)
        even_ref[block, :] = jnp.where(lower_half, q, 0.0).astype(BF16)
        odd_ref[block, :] = jnp.where(lower_half, 0.0, q).astype(BF16)

    def put_key(block, x, k_ref):
        k_ref[block, :] = dot(x, w_key[...]).astype(BF16)

    def put_value(block, x, even_ref, odd_ref):
        v = dot(x, w_value[...])
        even_ref[block, :] = jnp.where(lower_half, v, 1.0).astype(BF16)
        odd_ref[block, :] = jnp.where(lower_half, 1.0, v).astype(BF16)

    def attend(block, x, q_refs, k_ref, v_refs):
        def lanes(h):
            return slice(h // 2 * PAIRED, (h // 2 + 1) * PAIRED)

        def scores_of(h):
            return lax.dot_general(
                q_refs[h % 2][block, lanes(h)],
                k_ref[:, lanes(h)],
                (((1,), (1,)), ((), ())),
                preferred_element_type=F32,
            )

        scores = {h: scores_of(h) for h in range(AHEAD)}
        for h in range(HEADS):
            if h + AHEAD < HEADS:
                scores[h + AHEAD] = scores_of(h + AHEAD)
            s = scores.pop(h)
            expo = jnp.exp2(s - jnp.max(s, axis=1, keepdims=True)).astype(BF16)
            result = dot(expo, v_refs[h % 2][:, lanes(h)])
            if h % 2 == 0:
                even = result
            else:
                total = jnp.where(half, even, result)
                weight = pltpu.roll(jnp.where(half, result, even), HEAD_DIM, 1)
                context[block, lanes(h)] = (total / weight).astype(BF16)
        mixed = x.astype(F32) + dot(context[block, :], w_out[...])
        center = mixed - jnp.mean(mixed, axis=-1, keepdims=True)
        spread = jnp.mean(center * center, axis=-1, keepdims=True)
        return (center * lax.rsqrt(spread + 1e-06) * gain_ref[...][None]).astype(BF16)

    for load in loads[5:]:
        load.wait()
    for i in range(sends):
        to_fast(i).wait_recv()
    every = slice(0, tok)
    x = jnp.where(has_fast, from_fast[...], own[...])
    x_u[...] = x
    put_key(every, x, k_u)
    put_value(every, x, v_even_u, v_odd_u)
    put_query(every, x, q_even_u, q_odd_u)

    def back_to_fast(i):
        block = rows_of(i, ROWS)
        return remote(normed_u.at[block], back_fast.at[block], send_back_sem.at[0, i], recv_back_fast_sem.at[i], fast_id)

    def back_to_slow(i):
        block = rows_of(i, ROWS)
        return remote(normed_w.at[block], back_slow.at[block], send_back_sem.at[1, i], recv_back_slow_sem.at[i], slow_id)

    for i in range(steps):
        for part in range(i * ROWS // SEND_ROWS, (i + 1) * ROWS // SEND_ROWS):
            to_slow(part).wait_recv()
        block = slice(i * ROWS, (i + 1) * ROWS)
        x = jnp.where(has_slow, from_slow[block, :], own[block, :])
        put_query(block, x, q_even_w, q_odd_w)
        put_key(block, x, k_w)
        put_value(block, x, v_even_w, v_odd_w)
        normed_w[block, :] = attend(block, x, (q_even_w, q_odd_w), k_u, (v_even_u, v_odd_u))
        back_to_slow(i).start()

    for i in range(steps):
        block = slice(i * ROWS, (i + 1) * ROWS)
        normed_u[block, :] = attend(block, x_u[block, :], (q_even_u, q_odd_u), k_w, (v_even_w, v_odd_w))
        back_to_fast(i).start()

    for copy in conf_copies():
        copy.wait()
    parts = jnp.concatenate(
        [conf_fast[0:1, :], conf_slow[1:2, :], conf_out[2:4, :], jnp.zeros((4, tok), F32)], axis=0
    )
    weight = jnp.sum(parts, axis=0, keepdims=True)
    shares = jnp.transpose(parts / jnp.maximum(weight, 1.0))

    for i in range(steps):
        block = slice(i * ROWS, (i + 1) * ROWS)
        back_to_fast(i).wait_recv()
        back_to_slow(i).wait_recv()
        s = shares[block, :]
        merged = s[:, 0:1] * back_fast[block, :].astype(F32)
        merged += s[:, 1:2] * back_slow[block, :].astype(F32)
        merged += s[:, 2:3] * normed_u[block, :].astype(F32)
        merged += s[:, 3:4] * normed_w[block, :].astype(F32)
        merged_ref[block, :] = merged.astype(BF16)

    for i in range(sends):
        to_fast(i).wait_send()
        to_slow(i).wait_send()
    for i in range(steps):
        back_to_fast(i).wait_send()
        back_to_slow(i).wait_send()


def merged_normed(mesh_shape, pair_list, confidence, tokens, w_embed, w_query, w_key, w_value, w_out, norm_gain):
    tok = tokens.shape[1]
    width = w_embed.shape[1]
    in_hbm = pl.BlockSpec(memory_space=pl.ANY)
    operands = (pair_list, confidence, norm_gain, tokens, w_embed, w_query, w_key, w_value, w_out)
    return pl.pallas_call(
        functools.partial(kernel, mesh_shape),
        out_shape=jax.ShapeDtypeStruct((tok, width), BF16),
        in_specs=[in_hbm] * len(operands),
        out_specs=pl.BlockSpec(memory_space=pltpu.VMEM),
        scratch_shapes=[
            pltpu.SMEM(pair_list.shape, jnp.int32),
            pltpu.VMEM(confidence.shape, jnp.int32),
            pltpu.VMEM(norm_gain.shape, F32),
            pltpu.VMEM(tokens.shape[1:], BF16),
            pltpu.VMEM(w_embed.shape, BF16),
            pltpu.VMEM(w_query.shape, BF16),
            pltpu.VMEM(w_key.shape, BF16),
            pltpu.VMEM(w_value.shape, BF16),
            pltpu.VMEM(w_out.shape, BF16),
        ]
        + [pltpu.VMEM((tok, width), BF16)] * 19
        + [pltpu.VMEM((8, tok), F32)] * 3
        + [
            pltpu.SemaphoreType.DMA((len(operands),)),
            pltpu.SemaphoreType.DMA((2, tok // SEND_ROWS)),
            pltpu.SemaphoreType.DMA((tok // SEND_ROWS,)),
            pltpu.SemaphoreType.DMA((tok // SEND_ROWS,)),
            pltpu.SemaphoreType.DMA((2, tok // ROWS)),
            pltpu.SemaphoreType.DMA((tok // ROWS,)),
            pltpu.SemaphoreType.DMA((tok // ROWS,)),
            pltpu.SemaphoreType.DMA((4,)),
        ],
        compiler_params=pltpu.CompilerParams(
            collective_id=0, has_side_effects=True, vmem_limit_bytes=48 * 2**20
        ),
        name="pair_attention",
    )(*(pltpu.with_memory_space_constraint(a, pltpu.HBM) for a in operands))


def solution(mesh):
    mesh_shape = (mesh.shape["group"], mesh.shape["dev"])

    def on_device(
        tokens, pair_list, confidence, w_embed, w_query, w_key, w_value, w_out, norm_gain, w_head
    ):
        merged = merged_normed(
            mesh_shape, pair_list, confidence, tokens, w_embed, w_query, w_key, w_value, w_out, norm_gain
        )
        return dot(merged, w_head).astype(BF16)[None]

    along = ("group", "dev")
    in_specs = (P(along, None, None), P(along, None), P(along, None, None)) + (P(),) * 7
    return jax.shard_map(
        on_device, mesh=mesh, in_specs=in_specs, out_specs=P(along, None, None), check_vma=False
    )
```

time: 66.5 us -> 39.4 us (0.59)
  the two profiles are of different devices: /device:TPU:1 before, /device:TPU:0 now
where the time goes in v2:
time: 39.4 us; the launch traced here: 39.3 us
  Pallas kernels  34.9 us (89%)
  matrix products  4.42 us (11%)
    pallas_call x1, Pallas kernels, merged_normed(): pl.pallas_call(functools.partial(kernel, mesh_shape), out_shape=jax.Shape...  34.9 us
    dot_general x1, matrix products, dot(): return jnp.dot(a, b, preferred_element_type=F32)  4.42 us

profile of v2, /device:TPU:0, one launch (start us, length us, event | category | flops | bytes accessed | tf_op | source)
XLA Modules:
  0.0 39.3 jit_solution(2935623047077685294)
XLA Ops:
  0.0 0.0 copy-start
  0.0 34.9 %pair_attention.1 = bf16[512,768]{1,0:T(8,128)(2,1)S(1)} custom-call(s32[1,2]{1,0:T(1,128)} %pair_hbm.1, s32[1,2,512]{2,1,0:T(2,128)} %conf_hbm.1, f32[768]{0:T(1024)} %gain_hbm.1, bf16[1,512,1024]{2,1,0:T(8,128)(2,1)} %tokens_hbm.1, bf16[1024,768]{1,0:T(8,128)(2,1)} %w_embed_hbm.1, bf16[768,768]{1,0:T(8,128)(2,1)} %w_query_hbm.1, ...), custom_call_target="tpu_custom_call" | custom-call | tf_op jit(solution)/shard_map/pair_attention/pallas_call | solution.py:291
  34.9 0.0 copy-done
  34.9 4.4 %fusion = bf16[1,512,3456]{2,1,0:T(8,128)(2,1)} fusion(bf16[512,768]{1,0:T(8,128)(2,1)S(1)} %pair_attention.1, bf16[768,3456]{1,0:T(8,128)(2,1)S(1)} %copy-done), kind=kOutput, calls=%fused_computation.1 | convolution fusion | flops 2719678464 | bytes 9633792 | tf_op jit(solution)/shard_map/dot_general | solution.py:23
Async XLA Ops:
  0.0 34.9 %copy-start = (bf16[768,3456]{1,0:T(8,128)(2,1)S(1)}, bf16[768,3456]{1,0:T(8,128)(2,1)}, u32[]{:S(2)}) copy-start(bf16[768,3456]{1,0:T(8,128)(2,1)} %param.19) | copy-start | bytes 15925252

commit v3 on v2

--- a/solution.py
+++ b/solution.py
@@ -15,8 +15,12 @@
 BF16 = jnp.bfloat16
 F32 = jnp.float32
 SEND_ROWS = 128
-ROWS = 256
-AHEAD = 2
+W_BLOCKS = ((0, 128), (128, 256), (256, 384), (384, 512))
+U_BLOCKS = ((0, 256), (256, 512))
+HEAD_BLOCKS = ((0, 256), (256, 384))
+HEAD_ROWS = 384
+HEAD_TILE = 512
+FINISH_TILE = 1152
 
 
 def dot(a, b):
@@ -34,7 +38,10 @@
     w_key_hbm,
     w_value_hbm,
     w_out_hbm,
+    w_head_hbm,
     merged_ref,
+    head_ref,
+    w_head,
     pair_ref,
     conf_ref,
     gain_ref,
@@ -85,7 +92,7 @@
     slow_id = (lax.div(slow, n_dev), lax.rem(slow, n_dev))
     tok = own.shape[0]
     sends = tok // SEND_ROWS
-    steps = tok // ROWS
+    chained = jnp.logical_and(slow != 0, me != 0)
 
     def rows_of(step, size):
         return pl.ds(step * size, size)
@@ -94,8 +101,9 @@
         pltpu.make_async_copy(src, dst, load_sem.at[i])
         for i, (src, dst) in enumerate(
             (
+                (tokens_hbm.at[0, 0:SEND_ROWS], tokens.at[0:SEND_ROWS]),
                 (w_embed_hbm, w_embed),
-                (tokens_hbm.at[0], tokens),
+                (tokens_hbm.at[0, SEND_ROWS:tok], tokens.at[SEND_ROWS:tok]),
                 (pair_hbm, pair_ref),
                 (conf_hbm, conf_ref),
                 (gain_hbm, gain_ref),
@@ -103,15 +111,20 @@
                 (w_value_hbm, w_value),
                 (w_query_hbm, w_query),
                 (w_out_hbm, w_out),
+                (w_head_hbm, w_head),
             )
         )
     ]
-    for load in loads[:5]:
+    for load in loads[:6]:
         load.start()
 
     barrier = pltpu.get_barrier_semaphore()
     pl.semaphore_signal(barrier, inc=1, device_id=fast_id, device_id_type=MESH)
-    pl.semaphore_signal(barrier, inc=1, device_id=slow_id, device_id_type=MESH)
+
+    @pl.when(chained)
+    def _():
+        pl.semaphore_signal(barrier, inc=1, device_id=slow_id, device_id_type=MESH)
+
 
     def remote(src, dst, send, recv, target):
         return pltpu.make_async_remote_copy(
@@ -131,26 +144,42 @@
         block = rows_of(i, SEND_ROWS)
         return remote(own.at[block], from_slow.at[block], send_sem.at[1, i], recv_slow_sem.at[i], slow_id)
 
-    def conf_copies():
-        return (
-            remote(conf_out, conf_fast, conf_sem.at[0], conf_sem.at[1], fast_id),
-            remote(conf_out, conf_slow, conf_sem.at[2], conf_sem.at[3], slow_id),
-        )
+    def conf_to_fast():
+        return remote(conf_out, conf_fast, conf_sem.at[0], conf_sem.at[1], fast_id)
+
+    def conf_to_slow():
+        return remote(conf_out, conf_slow, conf_sem.at[2], conf_sem.at[3], slow_id)
 
     for load in loads[:2]:
         load.wait()
-    for load in loads[5:]:
+    for load in loads[6:]:
         load.start()
     for begin, end in ((0, SEND_ROWS), (SEND_ROWS, tok)):
+        if begin > 0:
+            loads[2].wait()
         own[begin:end, :] = dot(tokens[begin:end, :], w_embed[...]).astype(BF16)
         if begin == 0:
-            pl.semaphore_wait(barrier, 2)
-        for i in range(begin // SEND_ROWS, end // SEND_ROWS):
-            to_slow(i).start()
+
+            @pl.when(chained)
+            def _():
+                pl.semaphore_wait(barrier, 2)
+
+            @pl.when(jnp.logical_not(chained))
+            def _():
+                pl.semaphore_wait(barrier, 1)
+                from_slow[...] = jnp.zeros_like(from_slow)
+                back_slow[...] = jnp.zeros_like(back_slow)
+                conf_slow[...] = jnp.zeros_like(conf_slow)
+
+        @pl.when(chained)
+        def _(begin=begin, end=end):
+            for i in range(begin // SEND_ROWS, end // SEND_ROWS):
+                to_slow(i).start()
+
         for i in range(begin // SEND_ROWS, end // SEND_ROWS):
             to_fast(i).start()
 
-    for load in loads[2:5]:
+    for load in loads[3:6]:
         load.wait()
     first, second = pair_ref[0, 0], pair_ref[0, 1]
     has_fast = jnp.logical_or(first == fast, second == fast)
@@ -172,8 +201,12 @@
         ],
         axis=0,
     )
-    for copy in conf_copies():
-        copy.start()
+    conf_to_fast().start()
+
+    @pl.when(chained)
+    def _():
+        conf_to_slow().start()
+
 
     lower_half = lax.broadcasted_iota(jnp.int32, (1, HEADS * HEAD_DIM), 1) % PAIRED < HEAD_DIM
     half = lax.broadcasted_iota(jnp.int32, (1, PAIRED), 1) < HEAD_DIM
@@ -191,7 +224,7 @@
         even_ref[block, :] = jnp.where(lower_half, v, 1.0).astype(BF16)
         odd_ref[block, :] = jnp.where(lower_half, 1.0, v).astype(BF16)
 
-    def attend(block, x, q_refs, k_ref, v_refs):
+    def attend(block, x, q_refs, k_ref, v_refs, ahead):
         def lanes(h):
             return slice(h // 2 * PAIRED, (h // 2 + 1) * PAIRED)
 
@@ -203,10 +236,10 @@
                 preferred_element_type=F32,
             )
 
-        scores = {h: scores_of(h) for h in range(AHEAD)}
+        scores = {h: scores_of(h) for h in range(ahead)}
         for h in range(HEADS):
-            if h + AHEAD < HEADS:
-                scores[h + AHEAD] = scores_of(h + AHEAD)
+            if h + ahead < HEADS:
+                scores[h + ahead] = scores_of(h + ahead)
             s = scores.pop(h)
             expo = jnp.exp2(s - jnp.max(s, axis=1, keepdims=True)).astype(BF16)
             result = dot(expo, v_refs[h % 2][:, lanes(h)])
@@ -221,7 +254,7 @@
         spread = jnp.mean(center * center, axis=-1, keepdims=True)
         return (center * lax.rsqrt(spread + 1e-06) * gain_ref[...][None]).astype(BF16)
 
-    for load in loads[5:]:
+    for load in loads[6:10]:
         load.wait()
     for i in range(sends):
         to_fast(i).wait_recv()
@@ -233,66 +266,106 @@
     put_query(every, x, q_even_u, q_odd_u)
 
     def back_to_fast(i):
-        block = rows_of(i, ROWS)
+        block = pl.ds(U_BLOCKS[i][0], U_BLOCKS[i][1] - U_BLOCKS[i][0])
         return remote(normed_u.at[block], back_fast.at[block], send_back_sem.at[0, i], recv_back_fast_sem.at[i], fast_id)
 
     def back_to_slow(i):
-        block = rows_of(i, ROWS)
+        block = pl.ds(W_BLOCKS[i][0], W_BLOCKS[i][1] - W_BLOCKS[i][0])
         return remote(normed_w.at[block], back_slow.at[block], send_back_sem.at[1, i], recv_back_slow_sem.at[i], slow_id)
 
-    for i in range(steps):
-        for part in range(i * ROWS // SEND_ROWS, (i + 1) * ROWS // SEND_ROWS):
-            to_slow(part).wait_recv()
-        block = slice(i * ROWS, (i + 1) * ROWS)
+    for i, (begin, end) in enumerate(W_BLOCKS):
+
+        @pl.when(chained)
+        def _(begin=begin, end=end):
+            for part in range(begin // SEND_ROWS, end // SEND_ROWS):
+                to_slow(part).wait_recv()
+
+        block = slice(begin, end)
         x = jnp.where(has_slow, from_slow[block, :], own[block, :])
         put_query(block, x, q_even_w, q_odd_w)
         put_key(block, x, k_w)
         put_value(block, x, v_even_w, v_odd_w)
-        normed_w[block, :] = attend(block, x, (q_even_w, q_odd_w), k_u, (v_even_u, v_odd_u))
-        back_to_slow(i).start()
-
-    for i in range(steps):
-        block = slice(i * ROWS, (i + 1) * ROWS)
-        normed_u[block, :] = attend(block, x_u[block, :], (q_even_u, q_odd_u), k_w, (v_even_w, v_odd_w))
+        normed_w[block, :] = attend(block, x, (q_even_w, q_odd_w), k_u, (v_even_u, v_odd_u), 512 // (end - begin))
+
+        @pl.when(chained)
+        def _(i=i):
+            back_to_slow(i).start()
+
+    for i, (begin, end) in enumerate(U_BLOCKS):
+        block = slice(begin, end)
+        normed_u[block, :] = attend(
+            block, x_u[block, :], (q_even_u, q_odd_u), k_w, (v_even_w, v_odd_w), 512 // (end - begin)
+        )
         back_to_fast(i).start()
 
-    for copy in conf_copies():
-        copy.wait()
+    loads[10].wait()
+    conf_to_fast().wait()
+
+    @pl.when(chained)
+    def _():
+        conf_to_slow().wait()
+
     parts = jnp.concatenate(
         [conf_fast[0:1, :], conf_slow[1:2, :], conf_out[2:4, :], jnp.zeros((4, tok), F32)], axis=0
     )
     weight = jnp.sum(parts, axis=0, keepdims=True)
     shares = jnp.transpose(parts / jnp.maximum(weight, 1.0))
 
-    for i in range(steps):
-        block = slice(i * ROWS, (i + 1) * ROWS)
-        back_to_fast(i).wait_recv()
-        back_to_slow(i).wait_recv()
+    fast_here, slow_here = 0, 0
+    for begin, end in HEAD_BLOCKS + ((HEAD_ROWS, tok),):
+        block = slice(begin, end)
+        while fast_here < len(U_BLOCKS) and U_BLOCKS[fast_here][0] < end:
+            back_to_fast(fast_here).wait_recv()
+            fast_here += 1
+        behind = slow_here
+        while slow_here < len(W_BLOCKS) and W_BLOCKS[slow_here][0] < end:
+            slow_here += 1
+
+        @pl.when(chained)
+        def _(behind=behind, slow_here=slow_here):
+            for i in range(behind, slow_here):
+                back_to_slow(i).wait_recv()
+
         s = shares[block, :]
         merged = s[:, 0:1] * back_fast[block, :].astype(F32)
         merged += s[:, 1:2] * back_slow[block, :].astype(F32)
         merged += s[:, 2:3] * normed_u[block, :].astype(F32)
         merged += s[:, 3:4] * normed_w[block, :].astype(F32)
-        merged_ref[block, :] = merged.astype(BF16)
+        merged = merged.astype(BF16)
+        if begin < HEAD_ROWS:
+            for left in range(0, w_head.shape[1], HEAD_TILE):
+                tile = slice(left, min(left + HEAD_TILE, w_head.shape[1]))
+                head_ref[block, tile] = dot(merged, w_head[:, tile]).astype(BF16)
+        else:
+            merged_ref[...] = merged
 
     for i in range(sends):
         to_fast(i).wait_send()
-        to_slow(i).wait_send()
-    for i in range(steps):
+    for i in range(len(U_BLOCKS)):
         back_to_fast(i).wait_send()
-        back_to_slow(i).wait_send()
-
-
-def merged_normed(mesh_shape, pair_list, confidence, tokens, w_embed, w_query, w_key, w_value, w_out, norm_gain):
+
+    @pl.when(chained)
+    def _():
+        for i in range(sends):
+            to_slow(i).wait_send()
+        for i in range(len(W_BLOCKS)):
+            back_to_slow(i).wait_send()
+
+
+def merged_normed(mesh_shape, pair_list, confidence, tokens, w_embed, w_query, w_key, w_value, w_out, norm_gain, w_head):
     tok = tokens.shape[1]
     width = w_embed.shape[1]
     in_hbm = pl.BlockSpec(memory_space=pl.ANY)
-    operands = (pair_list, confidence, norm_gain, tokens, w_embed, w_query, w_key, w_value, w_out)
+    operands = (pair_list, confidence, norm_gain, tokens, w_embed, w_query, w_key, w_value, w_out, w_head)
     return pl.pallas_call(
         functools.partial(kernel, mesh_shape),
-        out_shape=jax.ShapeDtypeStruct((tok, width), BF16),
+        out_shape=(
+            jax.ShapeDtypeStruct((tok - HEAD_ROWS, width), BF16),
+            jax.ShapeDtypeStruct((HEAD_ROWS, w_head.shape[1]), BF16),
+            jax.ShapeDtypeStruct(w_head.shape, BF16),
+        ),
         in_specs=[in_hbm] * len(operands),
-        out_specs=pl.BlockSpec(memory_space=pltpu.VMEM),
+        out_specs=[pl.BlockSpec(memory_space=pltpu.VMEM)] * 3,
         scratch_shapes=[
             pltpu.SMEM(pair_list.shape, jnp.int32),
             pltpu.VMEM(confidence.shape, jnp.int32),
@@ -307,32 +380,66 @@
         + [pltpu.VMEM((tok, width), BF16)] * 19
         + [pltpu.VMEM((8, tok), F32)] * 3
         + [
-            pltpu.SemaphoreType.DMA((len(operands),)),
+            pltpu.SemaphoreType.DMA((len(operands) + 1,)),
             pltpu.SemaphoreType.DMA((2, tok // SEND_ROWS)),
             pltpu.SemaphoreType.DMA((tok // SEND_ROWS,)),
             pltpu.SemaphoreType.DMA((tok // SEND_ROWS,)),
-            pltpu.SemaphoreType.DMA((2, tok // ROWS)),
-            pltpu.SemaphoreType.DMA((tok // ROWS,)),
-            pltpu.SemaphoreType.DMA((tok // ROWS,)),
+            pltpu.SemaphoreType.DMA((2, len(W_BLOCKS))),
+            pltpu.SemaphoreType.DMA((len(U_BLOCKS),)),
+            pltpu.SemaphoreType.DMA((len(W_BLOCKS),)),
             pltpu.SemaphoreType.DMA((4,)),
         ],
         compiler_params=pltpu.CompilerParams(
-            collective_id=0, has_side_effects=True, vmem_limit_bytes=48 * 2**20
+            collective_id=0, has_side_effects=True, vmem_limit_bytes=40 * 2**20
         ),
         name="pair_attention",
     )(*(pltpu.with_memory_space_constraint(a, pltpu.HBM) for a in operands))
 
 
+def finish_kernel(merged_ref, head_ref, w_head, out_ref, last, copy_sem):
+    copy = pltpu.make_async_copy(head_ref, out_ref.at[0, 0:HEAD_ROWS], copy_sem.at[0])
+    copy.start()
+    copies = [copy]
+    width = w_head.shape[1]
+    for i, left in enumerate(range(0, width, FINISH_TILE)):
+        tile = slice(left, min(left + FINISH_TILE, width))
+        last[:, tile] = dot(merged_ref[...], w_head[:, tile]).astype(BF16)
+        copy = pltpu.make_async_copy(
+            last.at[:, tile], out_ref.at[0, HEAD_ROWS : out_ref.shape[1], tile], copy_sem.at[1 + i]
+        )
+        copy.start()
+        copies.append(copy)
+    for copy in copies:
+        copy.wait()
+
+
+def finished(merged, head, w_head):
+    tok, width = merged.shape[0] + head.shape[0], w_head.shape[1]
+    return pl.pallas_call(
+        finish_kernel,
+        out_shape=jax.ShapeDtypeStruct((1, tok, width), BF16),
+        in_specs=[pl.BlockSpec(memory_space=pltpu.VMEM)] * 3,
+        out_specs=pl.BlockSpec(memory_space=pltpu.HBM),
+        scratch_shapes=[
+            pltpu.VMEM((merged.shape[0], width), BF16),
+            pltpu.SemaphoreType.DMA((1 + -(-width // FINISH_TILE),)),
+        ],
+        compiler_params=pltpu.CompilerParams(vmem_limit_bytes=16 * 2**20),
+        name="head_of_last_rows",
+    )(merged, head, w_head)
+
+
 def solution(mesh):
     mesh_shape = (mesh.shape["group"], mesh.shape["dev"])
 
     def on_device(
         tokens, pair_list, confidence, w_embed, w_query, w_key, w_value, w_out, norm_gain, w_head
     ):
-        merged = merged_normed(
-            mesh_shape, pair_list, confidence, tokens, w_embed, w_query, w_key, w_value, w_out, norm_gain
+        return finished(
+            *merged_normed(
+                mesh_shape, pair_list, confidence, tokens, w_embed, w_query, w_key, w_value, w_out, norm_gain, w_head
+            )
         )
-        return dot(merged, w_head).astype(BF16)[None]
 
     along = ("group", "dev")
     in_specs = (P(along, None, None), P(along, None), P(along, None, None)) + (P(),) * 7

time: 39.4 us -> 33.2 us (0.84)
  the two profiles are of different devices: /device:TPU:0 before, /device:TPU:24 now
where the time goes in v3:
time: 33.2 us; the launch traced here: 33 us
  Pallas kernels  32.9 us (99%)
    pallas_call x1, Pallas kernels, merged_normed(): pl.pallas_call(functools.partial(kernel, mesh_shape), out_shape=(jax.Shap...  31 us
    pallas_call x1, Pallas kernels, finished(): pl.pallas_call(finish_kernel, out_shape=jax.ShapeDtypeStruct((1, tok, wid...  1.83 us

profile of v3, /device:TPU:24, one launch (start us, length us, event | category | flops | bytes accessed | tf_op | source)
XLA Modules:
  0.0 33.0 jit_solution(5153642372711213491)
XLA Ops:
  0.0 31.0 %pair_attention.1 = (bf16[128,768]{1,0:T(8,128)(2,1)S(1)}, bf16[384,3456]{1,0:T(8,128)(2,1)S(1)}, bf16[768,3456]{1,0:T(8,128)(2,1)S(1)}) custom-call(s32[1,2]{1,0:T(1,128)} %pair_hbm.1, s32[1,2,512]{2,1,0:T(2,128)} %conf_hbm.1, f32[768]{0:T(1024)} %gain_hbm.1, bf16[1,512,1024]{2,1,0:T(8,128)(2,1)} %tokens_hbm.1, bf16[1024,768]{1,0:T(8,128)(2,1)} %w_embed_hbm.1, ...), custom_call_target="tpu_custom_call" | custom-call | tf_op jit(solution)/shard_map/pair_attention/pallas_call | solution.py:360
  31.1 1.8 %head_of_last_rows.1 = bf16[1,512,3456]{2,1,0:T(8,128)(2,1)} custom-call(bf16[128,768]{1,0:T(8,128)(2,1)S(1)} %get-tuple-element.8.merged_ref, bf16[384,3456]{1,0:T(8,128)(2,1)S(1)} %get-tuple-element.9.head_ref, bf16[768,3456]{1,0:T(8,128)(2,1)S(1)} %get-tuple-element.10.w_head), custom_call_target="tpu_custom_call" | custom-call | tf_op jit(solution)/shard_map/head_of_last_rows/pallas_call | solution.py:418

commit v4 on v3

--- a/solution.py
+++ b/solution.py
@@ -15,7 +15,10 @@
 BF16 = jnp.bfloat16
 F32 = jnp.float32
 SEND_ROWS = 128
+EMBED_BLOCKS = ((0, 128), (128, 256), (256, 512))
+TAKE_BLOCKS = ((0, 256), (256, 512))
 W_BLOCKS = ((0, 128), (128, 256), (256, 384), (384, 512))
+EARLY_KEYS = 256
 U_BLOCKS = ((0, 256), (256, 512))
 HEAD_BLOCKS = ((0, 256), (256, 384))
 HEAD_ROWS = 384
@@ -55,21 +58,23 @@
     from_fast,
     from_slow,
     x_u,
+    x_w,
     q_even_u,
     q_odd_u,
     q_even_w,
     q_odd_w,
     k_u,
     k_w,
-    v_even_u,
-    v_odd_u,
-    v_even_w,
-    v_odd_w,
+    v_u,
+    v_w,
     context,
     normed_u,
     normed_w,
     back_fast,
     back_slow,
+    early_total,
+    early_weight,
+    early_top,
     conf_out,
     conf_fast,
     conf_slow,
@@ -154,8 +159,8 @@
         load.wait()
     for load in loads[6:]:
         load.start()
-    for begin, end in ((0, SEND_ROWS), (SEND_ROWS, tok)):
-        if begin > 0:
+    for begin, end in EMBED_BLOCKS:
+        if begin == SEND_ROWS:
             loads[2].wait()
         own[begin:end, :] = dot(tokens[begin:end, :], w_embed[...]).astype(BF16)
         if begin == 0:
@@ -219,51 +224,79 @@
     def put_key(block, x, k_ref):
         k_ref[block, :] = dot(x, w_key[...]).astype(BF16)
 
-    def put_value(block, x, even_ref, odd_ref):
-        v = dot(x, w_value[...])
-        even_ref[block, :] = jnp.where(lower_half, v, 1.0).astype(BF16)
-        odd_ref[block, :] = jnp.where(lower_half, 1.0, v).astype(BF16)
-
-    def attend(block, x, q_refs, k_ref, v_refs, ahead):
-        def lanes(h):
-            return slice(h // 2 * PAIRED, (h // 2 + 1) * PAIRED)
-
-        def scores_of(h):
+    def put_value(block, x, v_ref):
+        v_ref[block, :] = dot(x, w_value[...]).astype(BF16)
+
+    ones = jnp.ones((tok, PAIRED), BF16)
+
+    def lanes(h):
+        return slice(h // 2 * PAIRED, (h // 2 + 1) * PAIRED)
+
+    class Attention:
+        def __init__(self, block, x_ref, q_refs, k_ref, v_ref, keys):
+            self.block, self.keys = slice(*block), slice(*keys)
+            self.ahead = 512 * 512 // ((block[1] - block[0]) * (keys[1] - keys[0]))
+            self.x_ref, self.q_refs, self.k_ref, self.v_ref = x_ref, q_refs, k_ref, v_ref
+            self.scores = {h: self.scores_of(h) for h in range(self.ahead)}
+
+        def scores_of(self, h):
             return lax.dot_general(
-                q_refs[h % 2][block, lanes(h)],
-                k_ref[:, lanes(h)],
+                self.q_refs[h % 2][self.block, lanes(h)],
+                self.k_ref[self.keys, lanes(h)],
                 (((1,), (1,)), ((), ())),
                 preferred_element_type=F32,
             )
 
-        scores = {h: scores_of(h) for h in range(ahead)}
-        for h in range(HEADS):
-            if h + ahead < HEADS:
-                scores[h + ahead] = scores_of(h + ahead)
-            s = scores.pop(h)
-            expo = jnp.exp2(s - jnp.max(s, axis=1, keepdims=True)).astype(BF16)
-            result = dot(expo, v_refs[h % 2][:, lanes(h)])
-            if h % 2 == 0:
-                even = result
-            else:
-                total = jnp.where(half, even, result)
-                weight = pltpu.roll(jnp.where(half, result, even), HEAD_DIM, 1)
-                context[block, lanes(h)] = (total / weight).astype(BF16)
-        mixed = x.astype(F32) + dot(context[block, :], w_out[...])
-        center = mixed - jnp.mean(mixed, axis=-1, keepdims=True)
-        spread = jnp.mean(center * center, axis=-1, keepdims=True)
-        return (center * lax.rsqrt(spread + 1e-06) * gain_ref[...][None]).astype(BF16)
+        def heads(self, early=False, late=False):
+            for h in range(HEADS):
+                if h + self.ahead < HEADS:
+                    self.scores[h + self.ahead] = self.scores_of(h + self.ahead)
+                s = self.scores.pop(h)
+                top = jnp.max(s, axis=1, keepdims=True)
+                if early or late:
+                    top = jnp.broadcast_to(top, (s.shape[0], PAIRED))
+                    if late:
+                        before = early_top[h, self.block, :]
+                        top = jnp.maximum(top, before)
+                        scale = jnp.exp2(before - top)
+                    else:
+                        early_top[h, self.block, :] = top
+                    top = jnp.concatenate([top] * (s.shape[1] // PAIRED), axis=1)
+                expo = jnp.exp2(s - top).astype(BF16)
+                values = jnp.concatenate([self.v_ref[self.keys, lanes(h)], ones[: s.shape[1]]], axis=1)
+                result = dot(expo, values)
+                if h % 2 == 0:
+                    even, even_scale = result, scale if late else None
+                    continue
+                total = jnp.where(half, even[:, :PAIRED], result[:, :PAIRED])
+                weight = jnp.where(half, even[:, PAIRED:], result[:, PAIRED:])
+                if early:
+                    early_total[h // 2, self.block, :] = total
+                    early_weight[h // 2, self.block, :] = weight
+                    continue
+                if late:
+                    scale = jnp.where(half, even_scale, scale)
+                    total += early_total[h // 2, self.block, :] * scale
+                    weight += early_weight[h // 2, self.block, :] * scale
+                context[self.block, lanes(h)] = (total / weight).astype(BF16)
+
+        def normed(self):
+            mixed = self.x_ref[self.block, :].astype(F32) + dot(context[self.block, :], w_out[...])
+            center = mixed - jnp.mean(mixed, axis=-1, keepdims=True)
+            spread = jnp.mean(center * center, axis=-1, keepdims=True)
+            return (center * lax.rsqrt(spread + 1e-06) * gain_ref[...][None]).astype(BF16)
 
     for load in loads[6:10]:
         load.wait()
-    for i in range(sends):
-        to_fast(i).wait_recv()
-    every = slice(0, tok)
-    x = jnp.where(has_fast, from_fast[...], own[...])
-    x_u[...] = x
-    put_key(every, x, k_u)
-    put_value(every, x, v_even_u, v_odd_u)
-    put_query(every, x, q_even_u, q_odd_u)
+    for begin, end in TAKE_BLOCKS:
+        for i in range(begin // SEND_ROWS, end // SEND_ROWS):
+            to_fast(i).wait_recv()
+        block = slice(begin, end)
+        x = jnp.where(has_fast, from_fast[block, :], own[block, :])
+        x_u[block, :] = x
+        put_key(block, x, k_u)
+        put_value(block, x, v_u)
+        put_query(block, x, q_even_u, q_odd_u)
 
     def back_to_fast(i):
         block = pl.ds(U_BLOCKS[i][0], U_BLOCKS[i][1] - U_BLOCKS[i][0])
@@ -273,6 +306,14 @@
         block = pl.ds(W_BLOCKS[i][0], W_BLOCKS[i][1] - W_BLOCKS[i][0])
         return remote(normed_w.at[block], back_slow.at[block], send_back_sem.at[1, i], recv_back_slow_sem.at[i], slow_id)
 
+    def end_w(i, attention):
+        normed_w[attention.block, :] = attention.normed()
+
+        @pl.when(chained)
+        def _():
+            back_to_slow(i).start()
+
+    pending = None
     for i, (begin, end) in enumerate(W_BLOCKS):
 
         @pl.when(chained)
@@ -282,21 +323,33 @@
 
         block = slice(begin, end)
         x = jnp.where(has_slow, from_slow[block, :], own[block, :])
+        x_w[block, :] = x
         put_query(block, x, q_even_w, q_odd_w)
         put_key(block, x, k_w)
-        put_value(block, x, v_even_w, v_odd_w)
-        normed_w[block, :] = attend(block, x, (q_even_w, q_odd_w), k_u, (v_even_u, v_odd_u), 512 // (end - begin))
-
-        @pl.when(chained)
-        def _(i=i):
-            back_to_slow(i).start()
-
-    for i, (begin, end) in enumerate(U_BLOCKS):
-        block = slice(begin, end)
-        normed_u[block, :] = attend(
-            block, x_u[block, :], (q_even_u, q_odd_u), k_w, (v_even_w, v_odd_w), 512 // (end - begin)
+        put_value(block, x, v_w)
+        if pending is not None:
+            end_w(i - 1, pending)
+        pending = Attention((begin, end), x_w, (q_even_w, q_odd_w), k_u, v_u, (0, tok))
+        pending.heads()
+        if end == EARLY_KEYS:
+            early = Attention((0, tok), x_u, (q_even_u, q_odd_u), k_w, v_w, (0, EARLY_KEYS))
+            end_w(i, pending)
+            pending = None
+            early.heads(early=True)
+
+    attentions = []
+    for i, block in enumerate(U_BLOCKS):
+        attentions.append(
+            Attention(block, x_u, (q_even_u, q_odd_u), k_w, v_w, (EARLY_KEYS, tok))
         )
-        back_to_fast(i).start()
+        if i == 0:
+            end_w(len(W_BLOCKS) - 1, pending)
+        else:
+            normed_u[attentions[i - 1].block, :] = attentions[i - 1].normed()
+            back_to_fast(i - 1).start()
+        attentions[i].heads(late=True)
+    normed_u[attentions[-1].block, :] = attentions[-1].normed()
+    back_to_fast(len(U_BLOCKS) - 1).start()
 
     loads[10].wait()
     conf_to_fast().wait()
@@ -377,7 +430,9 @@
             pltpu.VMEM(w_value.shape, BF16),
             pltpu.VMEM(w_out.shape, BF16),
         ]
-        + [pltpu.VMEM((tok, width), BF16)] * 19
+        + [pltpu.VMEM((tok, width), BF16)] * 18
+        + [pltpu.VMEM((HEADS // 2, tok, PAIRED), F32)] * 2
+        + [pltpu.VMEM((HEADS, tok, PAIRED), F32)]
         + [pltpu.VMEM((8, tok), F32)] * 3
         + [
             pltpu.SemaphoreType.DMA((len(operands) + 1,)),

time: 33.2 us -> 34.2 us (1.030)
  Pallas kernels: 32.9 us -> 34 us
    pallas_call x1, Pallas kernels: 31 us -> 32.1 us  [merged_normed(): pl.pallas_call(functools.partial(kernel, mesh_shape), out_shape=(jax.Shap...]
where the time goes in v4:
time: 34.2 us; the launch traced here: 34.1 us
  Pallas kernels  34 us (99%)
    pallas_call x1, Pallas kernels, merged_normed(): pl.pallas_call(functools.partial(kernel, mesh_shape), out_shape=(jax.Shap...  32.1 us
    pallas_call x1, Pallas kernels, finished(): pl.pallas_call(finish_kernel, out_shape=jax.ShapeDtypeStruct((1, tok, wid...  1.83 us

profile of v4, /device:TPU:24, one launch (start us, length us, event | category | flops | bytes accessed | tf_op | source)
XLA Modules:
  0.0 34.1 jit_solution(12594784151168332529)
XLA Ops:
  0.0 32.1 %pair_attention.1 = (bf16[128,768]{1,0:T(8,128)(2,1)S(1)}, bf16[384,3456]{1,0:T(8,128)(2,1)S(1)}, bf16[768,3456]{1,0:T(8,128)(2,1)S(1)}) custom-call(s32[1,2]{1,0:T(1,128)} %pair_hbm.1, s32[1,2,512]{2,1,0:T(2,128)} %conf_hbm.1, f32[768]{0:T(1024)} %gain_hbm.1, bf16[1,512,1024]{2,1,0:T(8,128)(2,1)} %tokens_hbm.1, bf16[1024,768]{1,0:T(8,128)(2,1)} %w_embed_hbm.1, ...), custom_call_target="tpu_custom_call" | custom-call | tf_op jit(solution)/shard_map/pair_attention/pallas_call | solution.py:413
  32.1 1.8 %head_of_last_rows.1 = bf16[1,512,3456]{2,1,0:T(8,128)(2,1)} custom-call(bf16[128,768]{1,0:T(8,128)(2,1)S(1)} %get-tuple-element.8.merged_ref, bf16[384,3456]{1,0:T(8,128)(2,1)S(1)} %get-tuple-element.9.head_ref, bf16[768,3456]{1,0:T(8,128)(2,1)S(1)} %get-tuple-element.10.w_head), custom_call_target="tpu_custom_call" | custom-call | tf_op jit(solution)/shard_map/head_of_last_rows/pallas_call | solution.py:473

commit v5 on v4

--- a/solution.py
+++ b/solution.py
@@ -18,7 +18,6 @@
 EMBED_BLOCKS = ((0, 128), (128, 256), (256, 512))
 TAKE_BLOCKS = ((0, 256), (256, 512))
 W_BLOCKS = ((0, 128), (128, 256), (256, 384), (384, 512))
-EARLY_KEYS = 256
 U_BLOCKS = ((0, 256), (256, 512))
 HEAD_BLOCKS = ((0, 256), (256, 384))
 HEAD_ROWS = 384
@@ -72,9 +71,6 @@
     normed_w,
     back_fast,
     back_slow,
-    early_total,
-    early_weight,
-    early_top,
     conf_out,
     conf_fast,
     conf_slow,
@@ -102,13 +98,14 @@
     def rows_of(step, size):
         return pl.ds(step * size, size)
 
+    first_rows = EMBED_BLOCKS[0][1]
     loads = [
         pltpu.make_async_copy(src, dst, load_sem.at[i])
         for i, (src, dst) in enumerate(
             (
-                (tokens_hbm.at[0, 0:SEND_ROWS], tokens.at[0:SEND_ROWS]),
+                (tokens_hbm.at[0, 0:first_rows], tokens.at[0:first_rows]),
                 (w_embed_hbm, w_embed),
-                (tokens_hbm.at[0, SEND_ROWS:tok], tokens.at[SEND_ROWS:tok]),
+                (tokens_hbm.at[0, first_rows:tok], tokens.at[first_rows:tok]),
                 (pair_hbm, pair_ref),
                 (conf_hbm, conf_ref),
                 (gain_hbm, gain_ref),
@@ -160,7 +157,7 @@
     for load in loads[6:]:
         load.start()
     for begin, end in EMBED_BLOCKS:
-        if begin == SEND_ROWS:
+        if begin == first_rows:
             loads[2].wait()
         own[begin:end, :] = dot(tokens[begin:end, :], w_embed[...]).astype(BF16)
         if begin == 0:
@@ -247,37 +244,20 @@
                 preferred_element_type=F32,
             )
 
-        def heads(self, early=False, late=False):
+        def heads(self):
             for h in range(HEADS):
                 if h + self.ahead < HEADS:
                     self.scores[h + self.ahead] = self.scores_of(h + self.ahead)
                 s = self.scores.pop(h)
                 top = jnp.max(s, axis=1, keepdims=True)
-                if early or late:
-                    top = jnp.broadcast_to(top, (s.shape[0], PAIRED))
-                    if late:
-                        before = early_top[h, self.block, :]
-                        top = jnp.maximum(top, before)
-                        scale = jnp.exp2(before - top)
-                    else:
-                        early_top[h, self.block, :] = top
-                    top = jnp.concatenate([top] * (s.shape[1] // PAIRED), axis=1)
                 expo = jnp.exp2(s - top).astype(BF16)
                 values = jnp.concatenate([self.v_ref[self.keys, lanes(h)], ones[: s.shape[1]]], axis=1)
                 result = dot(expo, values)
                 if h % 2 == 0:
-                    even, even_scale = result, scale if late else None
+                    even = result
                     continue
                 total = jnp.where(half, even[:, :PAIRED], result[:, :PAIRED])
                 weight = jnp.where(half, even[:, PAIRED:], result[:, PAIRED:])
-                if early:
-                    early_total[h // 2, self.block, :] = total
-                    early_weight[h // 2, self.block, :] = weight
-                    continue
-                if late:
-                    scale = jnp.where(half, even_scale, scale)
-                    total += early_total[h // 2, self.block, :] * scale
-                    weight += early_weight[h // 2, self.block, :] * scale
                 context[self.block, lanes(h)] = (total / weight).astype(BF16)
 
         def normed(self):
@@ -331,23 +311,18 @@
             end_w(i - 1, pending)
         pending = Attention((begin, end), x_w, (q_even_w, q_odd_w), k_u, v_u, (0, tok))
         pending.heads()
-        if end == EARLY_KEYS:
-            early = Attention((0, tok), x_u, (q_even_u, q_odd_u), k_w, v_w, (0, EARLY_KEYS))
-            end_w(i, pending)
-            pending = None
-            early.heads(early=True)
 
     attentions = []
     for i, block in enumerate(U_BLOCKS):
         attentions.append(
-            Attention(block, x_u, (q_even_u, q_odd_u), k_w, v_w, (EARLY_KEYS, tok))
+            Attention(block, x_u, (q_even_u, q_odd_u), k_w, v_w, (0, tok))
         )
         if i == 0:
             end_w(len(W_BLOCKS) - 1, pending)
         else:
             normed_u[attentions[i - 1].block, :] = attentions[i - 1].normed()
             back_to_fast(i - 1).start()
-        attentions[i].heads(late=True)
+        attentions[i].heads()
     normed_u[attentions[-1].block, :] = attentions[-1].normed()
     back_to_fast(len(U_BLOCKS) - 1).start()
 
@@ -431,8 +406,6 @@
             pltpu.VMEM(w_out.shape, BF16),
         ]
         + [pltpu.VMEM((tok, width), BF16)] * 18
-        + [pltpu.VMEM((HEADS // 2, tok, PAIRED), F32)] * 2
-        + [pltpu.VMEM((HEADS, tok, PAIRED), F32)]
         + [pltpu.VMEM((8, tok), F32)] * 3
         + [
             pltpu.SemaphoreType.DMA((len(operands) + 1,)),

time: 34.2 us -> 32.9 us (0.962)
  Pallas kernels: 34 us -> 32.7 us
    pallas_call x1, Pallas kernels: 32.1 us -> 30.8 us  [merged_normed(): pl.pallas_call(functools.partial(kernel, mesh_shape), out_shape=(jax.Shap...]
where the time goes in v5:
time: 32.9 us; the launch traced here: 32.8 us
  Pallas kernels  32.7 us (99%)
    pallas_call x1, Pallas kernels, merged_normed(): pl.pallas_call(functools.partial(kernel, mesh_shape), out_shape=(jax.Shap...  30.8 us
    pallas_call x1, Pallas kernels, finished(): pl.pallas_call(finish_kernel, out_shape=jax.ShapeDtypeStruct((1, tok, wid...  1.83 us

profile of v5, /device:TPU:24, one launch (start us, length us, event | category | flops | bytes accessed | tf_op | source)
XLA Modules:
  0.0 32.8 jit_solution(3087343702613434976)
XLA Ops:
  0.0 30.8 %pair_attention.1 = (bf16[128,768]{1,0:T(8,128)(2,1)S(1)}, bf16[384,3456]{1,0:T(8,128)(2,1)S(1)}, bf16[768,3456]{1,0:T(8,128)(2,1)S(1)}) custom-call(s32[1,2]{1,0:T(1,128)} %pair_hbm.1, s32[1,2,512]{2,1,0:T(2,128)} %conf_hbm.1, f32[768]{0:T(1024)} %gain_hbm.1, bf16[1,512,1024]{2,1,0:T(8,128)(2,1)} %tokens_hbm.1, bf16[1024,768]{1,0:T(8,128)(2,1)} %w_embed_hbm.1, ...), custom_call_target="tpu_custom_call" | custom-call | tf_op jit(solution)/shard_map/pair_attention/pallas_call | solution.py:388
  30.8 1.8 %head_of_last_rows.1 = bf16[1,512,3456]{2,1,0:T(8,128)(2,1)} custom-call(bf16[128,768]{1,0:T(8,128)(2,1)S(1)} %get-tuple-element.8.merged_ref, bf16[384,3456]{1,0:T(8,128)(2,1)S(1)} %get-tuple-element.9.head_ref, bf16[768,3456]{1,0:T(8,128)(2,1)S(1)} %get-tuple-element.10.w_head), custom_call_target="tpu_custom_call" | custom-call | tf_op jit(solution)/shard_map/head_of_last_rows/pallas_call | solution.py:446

commit v6 on v5

--- a/solution.py
+++ b/solution.py
@@ -293,7 +293,6 @@
         def _():
             back_to_slow(i).start()
 
-    pending = None
     for i, (begin, end) in enumerate(W_BLOCKS):
 
         @pl.when(chained)
@@ -307,10 +306,23 @@
         put_query(block, x, q_even_w, q_odd_w)
         put_key(block, x, k_w)
         put_value(block, x, v_w)
-        if pending is not None:
-            end_w(i - 1, pending)
         pending = Attention((begin, end), x_w, (q_even_w, q_odd_w), k_u, v_u, (0, tok))
         pending.heads()
+        if end < tok:
+            end_w(i, pending)
+
+    loads[10].wait()
+    conf_to_fast().wait()
+
+    @pl.when(chained)
+    def _():
+        conf_to_slow().wait()
+
+    parts = jnp.concatenate(
+        [conf_fast[0:1, :], conf_slow[1:2, :], conf_out[2:4, :], jnp.zeros((4, tok), F32)], axis=0
+    )
+    weight = jnp.sum(parts, axis=0, keepdims=True)
+    shares = jnp.transpose(parts / jnp.maximum(weight, 1.0))
 
     attentions = []
     for i, block in enumerate(U_BLOCKS):
@@ -325,19 +337,6 @@
         attentions[i].heads()
     normed_u[attentions[-1].block, :] = attentions[-1].normed()
     back_to_fast(len(U_BLOCKS) - 1).start()
-
-    loads[10].wait()
-    conf_to_fast().wait()
-
-    @pl.when(chained)
-    def _():
-        conf_to_slow().wait()
-
-    parts = jnp.concatenate(
-        [conf_fast[0:1, :], conf_slow[1:2, :], conf_out[2:4, :], jnp.zeros((4, tok), F32)], axis=0
-    )
-    weight = jnp.sum(parts, axis=0, keepdims=True)
-    shares = jnp.transpose(parts / jnp.maximum(weight, 1.0))
 
     fast_here, slow_here = 0, 0
     for begin, end in HEAD_BLOCKS + ((HEAD_ROWS, tok),):

time: 32.9 us -> 32.5 us (0.988)
  Pallas kernels: 32.7 us -> 32.2 us
    pallas_call x1, Pallas kernels: 30.8 us -> 30.4 us  [merged_normed(): pl.pallas_call(functools.partial(kernel, mesh_shape), out_shape=(jax.Shap...]
where the time goes in v6:
time: 32.5 us; the launch traced here: 32.4 us
  Pallas kernels  32.2 us (99%)
    pallas_call x1, Pallas kernels, merged_normed(): pl.pallas_call(functools.partial(kernel, mesh_shape), out_shape=(jax.Shap...  30.4 us
    pallas_call x1, Pallas kernels, finished(): pl.pallas_call(finish_kernel, out_shape=jax.ShapeDtypeStruct((1, tok, wid...  1.83 us

profile of v6, /device:TPU:24, one launch (start us, length us, event | category | flops | bytes accessed | tf_op | source)
XLA Modules:
  0.0 32.4 jit_solution(14902642836002000227)
XLA Ops:
  0.0 30.4 %pair_attention.1 = (bf16[128,768]{1,0:T(8,128)(2,1)S(1)}, bf16[384,3456]{1,0:T(8,128)(2,1)S(1)}, bf16[768,3456]{1,0:T(8,128)(2,1)S(1)}) custom-call(s32[1,2]{1,0:T(1,128)} %pair_hbm.1, s32[1,2,512]{2,1,0:T(2,128)} %conf_hbm.1, f32[768]{0:T(1024)} %gain_hbm.1, bf16[1,512,1024]{2,1,0:T(8,128)(2,1)} %tokens_hbm.1, bf16[1024,768]{1,0:T(8,128)(2,1)} %w_embed_hbm.1, ...), custom_call_target="tpu_custom_call" | custom-call | tf_op jit(solution)/shard_map/pair_attention/pallas_call | solution.py:387
  30.4 1.8 %head_of_last_rows.1 = bf16[1,512,3456]{2,1,0:T(8,128)(2,1)} custom-call(bf16[128,768]{1,0:T(8,128)(2,1)S(1)} %get-tuple-element.8.merged_ref, bf16[384,3456]{1,0:T(8,128)(2,1)S(1)} %get-tuple-element.9.head_ref, bf16[768,3456]{1,0:T(8,128)(2,1)S(1)} %get-tuple-element.10.w_head), custom_call_target="tpu_custom_call" | custom-call | tf_op jit(solution)/shard_map/head_of_last_rows/pallas_call | solution.py:445
